TPU v7x, 1024 devices: a whole 8x8x8 slice. The times are simulated.
1024 devices in a mesh: dom: 4 (over x_lo, core), brick: 32 (over y, x_hi), slab: 8 (over z).
Axes of the slice: x: 8 (x_hi: 4, x_lo: 2; x = x_hi * 2 + x_lo), y: 8, z: 8, core: 2. Of those that a mesh axis runs over, the one named last changes fastest.
Arguments:
- heat_level: float32 [16, 512, 2048], P('dom', 'brick', 'slab'), may hold values from -6 to 6
- spread_ratio: float32 [16, 512, 2048], P('dom', 'brick', 'slab'), may hold values from 0.02 to 0.12
- stream_courant: float32 [16, 512, 2048], P('dom', 'brick', 'slab'), may hold values from 0 to 0.25
- interface_voxel: int32 [4, 32, 8, 2048], P('dom', 'brick', 'slab'), may hold values from 0 to 4095
- patch_holder_part: int32 [4, 32, 8, 2048, 1], P('dom', 'brick', 'slab'), may hold values from 0 to 31; in each aligned block of 2048 rows (0 to 2047, 2048 to 4095, ..., all dimensions but the last counted through in order) at most 128 rows name the same one
- patch_holder_voxel: int32 [4, 32, 8, 2048], P('dom', 'brick', 'slab'), may hold values from 0 to 4095
- interface_thermal_link: float32 [4, 32, 8, 2048], P('dom', 'brick', 'slab'), may hold values from 0.05 to 0.5
- interface_tally: int32 [4, 32, 8], P('dom', 'brick', 'slab'), may hold values from 1024 to 2048, as said below
Outputs:
- temperature_out: float32 [16, 512, 2048], P('dom', 'brick', 'slab')
Inputs may be any that keep to these rules, and one draw needn't show every extreme that they name: `patch_holder_part`: among the 2048 slots of one device no owner brick is named more than 128 times, and some device names one exactly 128 times. `interface_tally`: at least half of each device's slots are live; some device has all of them live.
All inputs are finite; a program needn't handle non-finite values.
Results may differ from a plain program's by a relative error of at most 0.0003.
Values sent between devices are 32-bit elements; how exact they have to be, the bound alone decides.
A program may use at most 32 MiB of HBM per device.

v0:
```python
import jax
import jax.numpy as jnp
from jax import lax
from jax.sharding import PartitionSpec as P

SWEEPS = 4


def extended(cells, sides, width):
    for axis, dim in sides:
        count = lax.axis_size(axis)
        ends = count - 1
        head = lax.slice_in_dim(cells, 0, width, axis=dim)
        tail = lax.slice_in_dim(cells, cells.shape[dim] - width, cells.shape[dim], axis=dim)
        cells = jnp.concatenate(
            [
                lax.ppermute(tail, axis, [(i, (i + 1) % count) for i in range(ends)]),
                cells,
                lax.ppermute(head, axis, [((i + 1) % count, i) for i in range(ends)]),
            ],
            axis=dim,
        )
    return cells


def spread(block, axis, source):
    block = jnp.where(lax.axis_index(axis) == source, block, jnp.zeros_like(block))
    return lax.psum(block, axis)


def neighbour_pattern(margin_extended, middle_value, spread_ratio, advect_speed):
    beside = (
        margin_extended[2:, 1:-1, 1:-1]
        + margin_extended[:-2, 1:-1, 1:-1]
        + margin_extended[1:-1, 2:, 1:-1]
        + margin_extended[1:-1, :-2, 1:-1]
        + margin_extended[1:-1, 1:-1, 2:]
        + margin_extended[1:-1, 1:-1, :-2]
    )
    return (
        middle_value
        + spread_ratio * (beside - 6.0 * middle_value)
        - advect_speed * (middle_value - margin_extended[1:-1, 1:-1, :-2])
    )


def iterate_single(heat_level_mesh, spread_ratio, advect_speed):
    margin_extended = extended(heat_level_mesh, (("brick", 1), ("slab", 2)), 1)
    margin_extended = jnp.pad(margin_extended, ((1, 1), (0, 0), (0, 0)))
    return neighbour_pattern(margin_extended, heat_level_mesh, spread_ratio, advect_speed)


def rank_slots(owner_brick, enabled_mask, bricks):
    face_total = owner_brick.shape[0]
    block_count = face_total // 128
    onehot = (jnp.arange(bricks)[:, None] == owner_brick[None, :]) & enabled_mask[None, :]
    onehot_blocks = onehot.astype(jnp.bfloat16).reshape(bricks, block_count, 128)
    lower_table = (jnp.arange(128)[:, None] <= jnp.arange(128)[None, :]).astype(jnp.bfloat16)
    within = jnp.einsum(
        "bkj,jl->bkl", onehot_blocks, lower_table, preferred_element_type=jnp.float32
    )
    block_totals = within[:, :, 127]
    before = jnp.cumsum(block_totals, axis=1) - block_totals
    running = within + before[:, :, None]
    chosen = jnp.sum(running * onehot_blocks.astype(jnp.float32), axis=0).reshape(face_total)
    return chosen.astype(jnp.int32) - 1


def body(
    heat_level,
    spread_ratio,
    stream_courant,
    interface_voxel,
    patch_holder_part,
    patch_holder_voxel,
    interface_thermal_link,
    interface_tally,
):
    region_total = lax.axis_size("dom")
    solid_index = region_total - 1
    dom_index = lax.axis_index("dom")
    is_solid = dom_index == solid_index
    solid_flag = is_solid.astype(jnp.float32)
    bricks = lax.axis_size("brick")
    heat_level_mesh = heat_level
    sheet_lines = heat_level_mesh.shape[1]
    sheet_columns = heat_level_mesh.shape[2]
    advect_speed = stream_courant * (1.0 - solid_flag)
    for repeat in range(SWEEPS):
        heat_level_mesh = iterate_single(heat_level_mesh, spread_ratio, advect_speed)
    liner_voxels = interface_voxel.reshape(-1)
    owner_brick = patch_holder_part.reshape(-1)
    land_target = patch_holder_voxel.reshape(-1)
    thermal_link = interface_thermal_link.reshape(-1)
    face_count = interface_tally.reshape(())
    face_total = liner_voxels.shape[0]
    slot_cap = 2 * face_total // bricks
    enabled_mask = (jnp.arange(face_total) < face_count) & jnp.logical_not(is_solid)
    slot_rank = rank_slots(owner_brick, enabled_mask, bricks)
    position_number = jnp.where(enabled_mask, owner_brick * slot_cap + slot_rank, bricks * slot_cap)
    liner_sheet = heat_level_mesh[0].reshape(-1)
    packed_rows = jnp.stack(
        [liner_sheet[liner_voxels], thermal_link, land_target.astype(jnp.float32)]
    )
    packet = (
        jnp.zeros((3, bricks * slot_cap + 1), jnp.float32)
        .at[:, position_number]
        .set(packed_rows)[:, : bricks * slot_cap]
    )
    packet = packet.reshape(3, bricks, slot_cap)
    grouped = lax.all_gather(packet[None], "dom", axis=0, tiled=True)
    arrived = lax.all_to_all(grouped, "brick", split_axis=2, concat_axis=2, tiled=True)
    inflow_temp = arrived[:, 0].reshape(-1)
    inflow_conduct = arrived[:, 1].reshape(-1)
    land_cell = arrived[:, 2].reshape(-1).astype(jnp.int32)
    solid_conduct = (
        jnp.zeros((sheet_lines * sheet_columns,), jnp.float32).at[land_cell].add(inflow_conduct)
    )
    solid_source = (
        jnp.zeros((sheet_lines * sheet_columns,), jnp.float32)
        .at[land_cell]
        .add(inflow_conduct * inflow_temp)
    )
    for repeat in range(SWEEPS):
        liner_previous = heat_level_mesh[0].reshape(-1)
        heat_level_mesh = iterate_single(heat_level_mesh, spread_ratio, advect_speed)
        summand_piece = (
            solid_flag * (solid_source - solid_conduct * liner_previous) / (1.0 + solid_conduct)
        )
        heat_level_mesh = heat_level_mesh.at[0].add(
            summand_piece.reshape(sheet_lines, sheet_columns)
        )
    liner_current = heat_level_mesh[0].reshape(-1)
    answer = liner_current[land_cell].reshape(region_total, bricks, slot_cap)
    sent_back = lax.all_to_all(answer, "brick", split_axis=1, concat_axis=1, tiled=True)
    chosen = spread(sent_back, "dom", solid_index)
    own_answer = lax.dynamic_index_in_dim(chosen, dom_index, 0, keepdims=False)
    wall_temp = own_answer.reshape(-1)[jnp.minimum(position_number, bricks * slot_cap - 1)]
    weight = jnp.where(enabled_mask, thermal_link, 0.0)
    fluid_link = jnp.zeros((sheet_lines * sheet_columns,), jnp.float32).at[liner_voxels].add(weight)
    fluid_input = (
        jnp.zeros((sheet_lines * sheet_columns,), jnp.float32)
        .at[liner_voxels]
        .add(weight * wall_temp)
    )
    sheet_current = heat_level_mesh[0].reshape(-1)
    refresh_step = (fluid_input - fluid_link * sheet_current) / (1.0 + fluid_link)
    return heat_level_mesh.at[0].add(refresh_step.reshape(sheet_lines, sheet_columns))


def solution(mesh):
    return jax.shard_map(
        body,
        mesh=mesh,
        in_specs=(
            P("dom", "brick", "slab"),
            P("dom", "brick", "slab"),
            P("dom", "brick", "slab"),
            P("dom", "brick", "slab", None),
            P("dom", "brick", "slab", None, None),
            P("dom", "brick", "slab", None),
            P("dom", "brick", "slab", None),
            P("dom", "brick", "slab"),
        ),
        out_specs=P("dom", "brick", "slab"),
        check_vma=False,
    )
```

profile of v0, /device:TPU:1, one launch (start us, length us, event | category | flops | bytes accessed | tf_op | source)
XLA Modules:
  0.0 645.6 jit_solution(16807507264926123174)
XLA Ops:
  7.4 4.9 collective-permute-start
  19.4 4.9 collective-permute-start.2
  25.8 4.9 collective-permute-done.3
  31.1 5.5 collective-permute-start.4
  37.9 3.9 collective-permute-done.5
  41.9 4.9 collective-permute-start.6
  48.2 6.2 collective-permute-done.7
  54.8 4.4 collective-permute-start.8
  60.5 3.9 collective-permute-done.9
  64.6 4.6 collective-permute-start.10
  83.1 4.3 collective-permute-start.14
  92.9 5.0 collective-permute-start.16
  99.3 11.8 %gather_fusion = f32[2048]{0:T(1024)S(1)} fusion(f32[4096]{0:T(1024)S(1)} %bitcast.53, s32[2048]{0:T(1024)S(1)} %broadcast_clamp_fusion.2), kind=kCustom, calls=%fused_computation | custom fusion | bytes 24576 | tf_op jit(solution)/shard_map/gather | solution.py:103
  111.5 6.1 scatter_custom_fusion
  121.3 16.7 %all_gather.3 = f32[4,3,32,128]{3,2,1,0:T(8,128)S(1)} all-gather(f32[1,3,32,128]{3,2,1,0:T(8,128)S(1)} %copy.52), channel_id=1, replica_groups=mesh['dom'=4,'brick'=32,'slab'=8] {'dom'}, dimensions={0}, use_global_device_ids=true | all-gather | bytes 245760 | tf_op jit(solution)/shard_map/all_gather | solution.py:111
  138.8 14.4 %all-to-all-start = ((f32[4,3,32,128]{3,0,1,2:T(4,128)}), f32[4,3,32,128]{3,0,1,2:T(4,128)S(1)}, u32[]{:S(2)}, u32[]{:S(2)}) async-start(f32[4,3,32,128]{3,0,1,2:T(4,128)} %copy.53), calls=%async_computation | async-start | bytes 393216 | tf_op jit(solution)/shard_map/all_to_all | solution.py:112
  153.3 4.0 collective-permute-start.18
  158.6 4.1 collective-permute-done.19
  165.0 96.9 %scatter_custom_fusion.2 = f32[4096]{0:T(1024)S(1)} fusion(s32[16384]{0:T(1024)S(1)} %bitcast.60, f32[16384]{0:T(1024)S(1)} %bitcast.59, f32[]{:T(128)} %constant.138.clone.1), kind=kCustom, calls=%fused_computation.230 | custom fusion | flops 16384 | bytes 16388 | tf_op jit(solution)/shard_map/scatter-add | solution.py:117
  261.9 96.9 %scatter_custom_fusion.1 = f32[4096]{0:T(1024)S(1)} fusion(s32[16384]{0:T(1024)S(1)} %bitcast.61, f32[16384]{0:T(1024)S(1)} %mul.162, f32[]{:T(128)} %constant.138.clone.1), kind=kCustom, calls=%fused_computation.232 | custom fusion | flops 16384 | bytes 16388 | tf_op jit(solution)/shard_map/scatter-add | solution.py:122
  358.9 25.0 %collective-permute-start.20 = (f32[4,1,256]{2,1,0:T(1,128)S(1)}, f32[4,1,256]{2,1,0:T(1,128)S(1)}, u32[]{:S(2)}, u32[]{:S(2)}) collective-permute-start(f32[4,1,256]{2,1,0:T(1,128)S(1)} %get-tuple-element.100), channel_id=1, source_target_pairs={{0,8},{8,16},{16,24},{24,32},{32,40},{40,48},{48,56},{56,64},{64,7... | collective-permute-start | bytes 12296 | tf_op jit(solution)/shard_map/ppermute | solution.py:17
  385.3 3.9 collective-permute-done.21
  389.3 4.5 collective-permute-start.22
  399.1 5.5 collective-permute-start.24
  406.0 3.9 collective-permute-done.25
  418.5 5.5 collective-permute-start.28
  437.9 90.5 %gather_fusion.1 = f32[16384]{0:T(1024)S(1)} fusion(f32[4096]{0:T(1024)S(1)} %bitcast.51, s32[16384]{0:T(1024)S(1)} %broadcast_clamp_fusion), kind=kCustom, calls=%fused_computation.1 | custom fusion | bytes 196608 | tf_op jit(solution)/shard_map/gather | solution.py:134
  528.5 20.4 %all_to_all.10 = f32[4,32,128]{2,0,1:T(4,128)S(1)} all-to-all(f32[4,32,128]{2,0,1:T(4,128)S(1)} %copy.57), channel_id=1, replica_groups=mesh['dom'=4,'brick'=32,'slab'=8] {'brick'}, dimensions={1} | all-to-all | bytes 131072 | tf_op jit(solution)/shard_map/all_to_all | solution.py:135
  549.6 53.4 %all-reduce.10.cloned.1.call-done = f32[4,32,128]{2,0,1:T(4,128)} async-done(((f32[4,32,128]{2,0,1:T(4,128)}), f32[4,32,128]{2,0,1:T(4,128)}) %all-reduce.10.cloned.1.call-update) | async-done | bytes 65552 | tf_op jit(solution)/shard_map/psum | solution.py:28
  603.8 11.8 %gather_fusion.2 = f32[2048]{0:T(1024)S(1)} fusion(f32[4096]{0:T(1024)S(1)} %bitcast.55, s32[2048]{0:T(1024)S(1)} %broadcast_clamp_fusion.1), kind=kCustom, calls=%fused_computation.2 | custom fusion | bytes 24576 | tf_op jit(solution)/shard_map/gather | solution.py:138
  615.6 11.2 %scatter_custom_fusion.3 = f32[4096]{0:T(1024)S(1)} fusion(s32[2048]{0:T(1024)S(1)} %bitcast.73, f32[2048]{0:T(1024)S(1)} %get-tuple-element.65, f32[]{:T(128)} %constant.138.clone.1), kind=kCustom, calls=%fused_computation.228 | custom fusion | flops 2048 | bytes 16388 | tf_op jit(solution)/shard_map/scatter-add | solution.py:144
  626.9 11.2 %scatter_custom_fusion.4 = f32[4096]{0:T(1024)S(1)} fusion(s32[2048]{0:T(1024)S(1)} %bitcast.74, f32[2048]{0:T(1024)S(1)} %get-tuple-element.66, f32[]{:T(128)} %constant.138.clone.1), kind=kCustom, calls=%fused_computation.226 | custom fusion | flops 2048 | bytes 16388 | tf_op jit(solution)/shard_map/scatter-add | solution.py:140
  (157 shorter events, 75.3 us)
Async XLA Ops:
  7.4 8.4 %collective-permute-start = (f32[4,1,256]{2,1,0:T(1,128)S(1)}, f32[4,1,256]{2,1,0:T(1,128)S(1)}, u32[]{:S(2)}, u32[]{:S(2)}) collective-permute-start(f32[4,1,256]{2,1,0:T(1,128)S(1)} %get-tuple-element.110), channel_id=1, source_target_pairs={{0,8},{8,16},{16,24},{24,32},{32,40},{40,48},{48,56},{56,64},{64,7... | collective-permute-start | bytes 12296 | tf_op jit(solution)/shard_map/ppermute | solution.py:17
  12.2 6.3 collective-permute-start.1
  19.4 6.4 collective-permute-start.2
  24.4 6.4 collective-permute-start.3
  31.1 6.8 %collective-permute-start.4 = (f32[4,1,256]{2,1,0:T(1,128)S(1)}, f32[4,1,256]{2,1,0:T(1,128)S(1)}, u32[]{:S(2)}, u32[]{:S(2)}) collective-permute-start(f32[4,1,256]{2,1,0:T(1,128)S(1)} %get-tuple-element.108), channel_id=1, source_target_pairs={{0,8},{8,16},{16,24},{24,32},{32,40},{40,48},{48,56},{56,64},{64,7... | collective-permute-start | bytes 12296 | tf_op jit(solution)/shard_map/ppermute | solution.py:17
  36.6 5.3 collective-permute-start.5
  41.9 6.3 collective-permute-start.6
  46.8 7.6 %collective-permute-start.7 = (f32[4,18,1]{2,1,0:T(8,128)S(1)}, f32[4,18,1]{2,1,0:T(8,128)S(1)}, u32[]{:S(2)}, u32[]{:S(2)}) collective-permute-start(f32[4,18,1]{2,1,0:T(8,128)S(1)} %get-tuple-element.85), channel_id=1, source_target_pairs={{1,0},{2,1},{3,2},{4,3},{5,4},{6,5},{7,6},{9,8},{10,9},{11,10},{12... | collective-permute-start | bytes 872 | tf_op jit(solution)/shard_map/ppermute | solution.py:19
  54.8 5.7 collective-permute-start.8
  59.2 5.3 collective-permute-start.9
  64.6 5.9 collective-permute-start.10
  69.1 4.9 collective-permute-start.11
  77.8 5.3 collective-permute-start.13
  83.1 5.6 collective-permute-start.14
  87.4 5.1 collective-permute-start.15
  92.9 60.3 %collective-permute-start.16 = (f32[4,1,256]{2,1,0:T(1,128)S(1)}, f32[4,1,256]{2,1,0:T(1,128)S(1)}, u32[]{:S(2)}, u32[]{:S(2)}) collective-permute-start(f32[4,1,256]{2,1,0:T(1,128)S(1)} %get-tuple-element.102), channel_id=1, source_target_pairs={{0,8},{8,16},{16,24},{24,32},{32,40},{40,48},{48,56},{56,64},{64,7... | collective-permute-start | bytes 12296 | tf_op jit(solution)/shard_map/ppermute | solution.py:17
  98.0 55.2 %collective-permute-start.17 = (f32[4,1,256]{2,1,0:T(1,128)S(1)}, f32[4,1,256]{2,1,0:T(1,128)S(1)}, u32[]{:S(2)}, u32[]{:S(2)}) collective-permute-start(f32[4,1,256]{2,1,0:T(1,128)S(1)} %get-tuple-element.103), channel_id=1, source_target_pairs={{8,0},{16,8},{24,16},{32,24},{40,32},{48,40},{56,48},{64,56},{72,6... | collective-permute-start | bytes 12296 | tf_op jit(solution)/shard_map/ppermute | solution.py:19
  138.8 26.0 %all-to-all-start = ((f32[4,3,32,128]{3,0,1,2:T(4,128)}), f32[4,3,32,128]{3,0,1,2:T(4,128)S(1)}, u32[]{:S(2)}, u32[]{:S(2)}) async-start(f32[4,3,32,128]{3,0,1,2:T(4,128)} %copy.53), calls=%async_computation | async-start | bytes 393216 | tf_op jit(solution)/shard_map/all_to_all | solution.py:112
  153.2 449.8 %all-reduce.10.cloned.1.call-start = ((), (), s32[]{:S(2)}) async-start(), calls=%async_computation.2 | async-start | bytes 131072 | tf_op jit(solution)/shard_map/psum | solution.py:28
  153.3 5.3 collective-permute-start.18
  157.3 5.4 collective-permute-start.19
  358.9 26.3 %collective-permute-start.20 = (f32[4,1,256]{2,1,0:T(1,128)S(1)}, f32[4,1,256]{2,1,0:T(1,128)S(1)}, u32[]{:S(2)}, u32[]{:S(2)}) collective-permute-start(f32[4,1,256]{2,1,0:T(1,128)S(1)} %get-tuple-element.100), channel_id=1, source_target_pairs={{0,8},{8,16},{16,24},{24,32},{32,40},{40,48},{48,56},{56,64},{64,7... | collective-permute-start | bytes 12296 | tf_op jit(solution)/shard_map/ppermute | solution.py:17
  383.9 5.3 collective-permute-start.21
  389.3 5.9 collective-permute-start.22
  393.8 4.9 collective-permute-start.23
  399.1 6.9 %collective-permute-start.24 = (f32[4,1,256]{2,1,0:T(1,128)S(1)}, f32[4,1,256]{2,1,0:T(1,128)S(1)}, u32[]{:S(2)}, u32[]{:S(2)}) collective-permute-start(f32[4,1,256]{2,1,0:T(1,128)S(1)} %get-tuple-element.98), channel_id=1, source_target_pairs={{0,8},{8,16},{16,24},{24,32},{32,40},{40,48},{48,56},{56,64},{64,7... | collective-permute-start | bytes 12296 | tf_op jit(solution)/shard_map/ppermute | solution.py:17
  404.6 5.3 collective-permute-start.25
  413.3 4.8 collective-permute-start.27
  418.5 6.8 %collective-permute-start.28 = (f32[4,1,256]{2,1,0:T(1,128)S(1)}, f32[4,1,256]{2,1,0:T(1,128)S(1)}, u32[]{:S(2)}, u32[]{:S(2)}) collective-permute-start(f32[4,1,256]{2,1,0:T(1,128)S(1)} %get-tuple-element.96), channel_id=1, source_target_pairs={{0,8},{8,16},{16,24},{24,32},{32,40},{40,48},{48,56},{56,64},{64,7... | collective-permute-start | bytes 12296 | tf_op jit(solution)/shard_map/ppermute | solution.py:17
  424.0 5.3 collective-permute-start.29
  429.4 4.9 collective-permute-start.30
  432.7 4.8 collective-permute-start.31
  (10 other events, 304.1 us)
Sparse Core Ops, SparseCore 0:
  549.7 53.2 all-reduce.9
where the time goes:
time: 647 us; the launch traced here: 646 us
  other arithmetic  222 us (34%)
  local copies, waits for them, and re-layouts  128 us (20%)
  starting transfers between devices  128 us (20%)
  waiting for transfers between devices  115 us (18%)
  blocking collectives  37.1 us (6%)
  between operations  15.1 us (2%)
    scatter-add x1, other arithmetic, body(): jnp.zeros((sheet_lines * sheet_columns,), jnp.float32).at[land_cell]  96.9 us
    scatter-add x1, other arithmetic, body(): solid_source = jnp.zeros((sheet_lines * sheet_columns,), jnp.float32).at[...  96.9 us
    ppermute x16, starting transfers between devices, extended(): lax.ppermute(tail, axis, [(i, (i + 1) % count) for i in range(ends)])  93 us
    gather x1, local copies, waits for them, and re-layouts, body(): answer = liner_current[land_cell].reshape(region_total, bricks, slot_cap)  90.5 us
    ppermute x16, waiting for transfers between devices, extended(): lax.ppermute(head, axis, [((i + 1) % count, i) for i in range(ends)])  59.3 us
    psum x1, waiting for transfers between devices, spread(): return lax.psum(block, axis)  53.4 us
    ppermute x16, starting transfers between devices, extended(): lax.ppermute(head, axis, [((i + 1) % count, i) for i in range(ends)])  20.9 us
    all_to_all x1, blocking collectives, body(): lax.all_to_all(answer, 'brick', split_axis=1, concat_axis=1, tiled=True)  20.4 us
  transfers between devices with their start and end apart: 34, of which 17 were waited for; matrix products, arithmetic and copies ran while one was open for 4% of the time, Pallas kernels for 0%

commit v1 on v0

v1 whole, which is shorter than its diff:
```python
import functools
import math

import jax
import jax.numpy as jnp
from jax import lax
from jax.experimental import pallas as pl
from jax.experimental.pallas import tpu as pltpu
from jax.sharding import PartitionSpec as P

SWEEPS = 4
W = 4
CAP = 128
LAYERS, ROWS, COLS = 4, 16, 256
XR, XC = ROWS + 8, COLS + 128
PARTS = 7
STEPS = ((-1, 0), (1, 0), (0, -1), (0, 1), (-1, -1), (-1, 1), (1, -1), (1, 1))
MESH = pl.DeviceIdType.MESH
F32, BF16, I32 = jnp.float32, jnp.bfloat16, jnp.int32
NT = (((1,), (1,)), ((), ()))
NN = (((1,), (0,)), ((), ()))


def iota(shape, dim):
    return lax.broadcasted_iota(I32, shape, dim)


def dot(a, b, dims):
    return lax.dot_general(a, b, dims, preferred_element_type=F32)


def split2(x):
    high = x.astype(BF16).astype(F32)
    return high, x - high


def kernel(
    nd, nb, ns,
    heat, ratio, courant, voxel_h, owner_h, target_h, link_h, tally,
    out,
    ua, ub, rx, cx, gx, sx,
    voxel, owner, target, link,
    ysend, zsend, yst, zst, dst8,
    uy, uz, udg, gy, gz, gdg, sy, sz, sdg,
    hot, owner_hot, prefix, meta_a, meta_b,
    cell_y, cell_z, link_p, q_rows, wall_rows, hsum,
    meta_send, q_send, meta_recv, q_recv, ans_send, wall_recv,
    in_sem, slot_sem, out_sem,
    a_send, a_recv, u_send, u_recv, g_send, g_recv, s_send, s_recv,
    meta_ssem, meta_rsem, q_ssem, q_rsem, ans_ssem, ans_rsem,
):
    dom, brick, slab = lax.axis_index("dom"), lax.axis_index("brick"), lax.axis_index("slab")
    last = nd - 1
    solid = dom == last
    rows_in = last * nb

    own = (slice(None), pl.ds(0, ROWS), pl.ds(0, COLS))
    fields = [
        pltpu.make_async_copy(h, x.at[own], in_sem.at[i])
        for i, (h, x) in enumerate(((heat, ua), (ratio, rx), (courant, cx)))
    ]
    slots = [
        pltpu.make_async_copy(h, v, slot_sem.at[i])
        for i, (h, v) in enumerate(((owner_h, owner), (voxel_h, voxel), (target_h, target), (link_h, link)))
    ]
    for copy in fields:
        copy.start()
    for copy in slots:
        copy.start()

    def neighbour(step):
        db, dz = step
        return (dom, lax.rem(brick + db + nb, nb), lax.rem(slab + dz + ns, ns))

    barrier = pltpu.get_barrier_semaphore()
    for step in STEPS:
        pl.semaphore_signal(barrier, inc=1, device_id=neighbour(step), device_id_type=MESH)

    @pl.when(solid)
    def _():
        def greet(i, _):
            for d in range(last):
                to = lax.rem(brick + i, nb)
                pl.semaphore_signal(barrier, inc=1, device_id=(d, to, slab), device_id_type=MESH)
            return 0

        lax.fori_loop(0, nb, greet, 0)

    @pl.when(jnp.logical_not(solid))
    def _():
        def greet(i, _):
            to = lax.rem(brick + i, nb)
            pl.semaphore_signal(barrier, inc=1, device_id=(last, to, slab), device_id_type=MESH)
            return 0

        lax.fori_loop(0, nb, greet, 0)

    gas = jnp.where(solid, 0.0, 1.0).astype(F32)
    more_b = jnp.where(brick < nb - 1, 1.0, 0.0).astype(F32)
    less_b = jnp.where(brick > 0, 1.0, 0.0).astype(F32)
    more_z = jnp.where(slab < ns - 1, 1.0, 0.0).astype(F32)
    less_z = jnp.where(slab > 0, 1.0, 0.0).astype(F32)

    for copy in fields:
        copy.wait()
    lane16 = iota((ROWS, 128), 1)
    first, final = jnp.zeros((ROWS, 128), F32), jnp.zeros((ROWS, 128), F32)
    packed = jnp.zeros((ROWS, 128), F32)
    for l in range(LAYERS):
        c = cx[l, 0:ROWS, 0:COLS] * gas
        cx[l, 0:ROWS, 0:COLS] = c
        u, r = ua[l, 0:ROWS, 0:COLS], rx[l, 0:ROWS, 0:COLS]
        ysend[0, l] = jnp.concatenate([u[0:W], r[0:W]], axis=0)
        ysend[1, l] = jnp.concatenate([u[ROWS - W:], r[ROWS - W:]], axis=0)
        ysend[0, LAYERS + l // 2, (l % 2) * W:(l % 2) * W + W, :] = c[0:W]
        ysend[1, LAYERS + l // 2, (l % 2) * W:(l % 2) * W + W, :] = c[ROWS - W:]
        for a, x in enumerate((u, r, c)):
            g = (l * 3 + a) * W
            head = pltpu.roll(x[:, 0:128], g, 1) if g else x[:, 0:128]
            tail = pltpu.roll(x[:, 128:256], (64 + g + W) % 128, 1)
            packed = jnp.where((lane16 >= g) & (lane16 < g + W), head, packed)
            packed = jnp.where((lane16 >= 64 + g) & (lane16 < 64 + g + W), tail, packed)
    zsend[...] = packed

    count = jnp.where(solid, len(STEPS) + rows_in, len(STEPS) + nb)
    pl.semaphore_wait(barrier, count)

    def halo_copies(sources, landings, ssem, rsem):
        return [
            pltpu.make_async_remote_copy(
                src_ref=sources[m], dst_ref=landings[m], send_sem=ssem.at[m], recv_sem=rsem.at[m],
                device_id=neighbour(step), device_id_type=MESH,
            )
            for m, step in enumerate(STEPS)
        ]

    low, high = zsend.at[pl.ds(0, 8)], zsend.at[pl.ds(ROWS - 8, 8)]
    a_copies = halo_copies(
        [ysend.at[0], ysend.at[1], zsend, zsend, low, low, high, high],
        [yst.at[0], yst.at[1], zst.at[0], zst.at[1]] + [dst8.at[i] for i in range(4)],
        a_send, a_recv,
    )
    for copy in a_copies:
        copy.start()

    def sheet_copies(x, y, z, d, ssem, rsem):
        def part(r0, rn, c0, cn):
            return x.at[:, pl.ds(r0, rn), pl.ds(c0, cn)]

        return halo_copies(
            [
                part(0, 8, 0, COLS), part(ROWS - 8, 8, 0, COLS),
                part(0, ROWS, 0, 128), part(0, ROWS, COLS - 128, 128),
                part(0, 8, 0, 128), part(0, 8, COLS - 128, 128),
                part(ROWS - 8, 8, 0, 128), part(ROWS - 8, 8, COLS - 128, 128),
            ],
            [y.at[0], y.at[1], z.at[0], z.at[1]] + [d.at[i] for i in range(4)],
            ssem, rsem,
        )

    u_copies = sheet_copies(ua, uy, uz, udg, u_send, u_recv)
    g_copies = sheet_copies(gx, gy, gz, gdg, g_send, g_recv)
    s_copies = sheet_copies(sx, sy, sz, sdg, s_send, s_recv)

    row8 = iota((8, COLS), 0)
    row8n = iota((8, 128), 0)
    lane8 = iota((8, 128), 1)

    def sides(right, left, lanes):
        return jnp.where(lanes < W, right * more_z, jnp.where(lanes >= 128 - W, left * less_z, 0.0))

    def unpack(x, y, z, d, layers):
        for l in range(layers):
            x[l, ROWS:XR, 0:COLS] = jnp.where(row8 < W, y[0, l] * more_b, y[1, l] * less_b)
            x[l, 0:ROWS, COLS:XC] = sides(z[0, l], z[1, l], lane16)
            right = jnp.where(row8n < W, d[0, l] * more_b, d[2, l] * less_b)
            left = jnp.where(row8n < W, d[1, l] * more_b, d[3, l] * less_b)
            x[l, ROWS:XR, COLS:XC] = sides(right, left, lane8)

    @pl.when(jnp.logical_not(solid))
    def _():
        for copy in slots:
            copy.wait()
        live_count = tally[0]
        a, b = iota((128, 128), 0), iota((128, 128), 1)
        before = jnp.concatenate([jnp.where(a < b, 1.0, 0.0), jnp.ones((128, 128), F32)], axis=1).astype(BF16)
        bricks = iota((nb, 128), 0)
        lanes = iota((1, 128), 1)
        groups = owner.shape[0]

        def mark(j, _):
            live = j * 128 + lanes < live_count
            named = jnp.where(live, owner[pl.ds(j, 1), :], nb)
            owner_hot[pl.ds(pl.multiple_of(j * nb, nb), nb), :] = jnp.where(bricks == named, 1.0, 0.0)
            return 0

        lax.fori_loop(0, groups, mark, 0)
        prefix[...] = dot(owner_hot[...].astype(BF16), before, NN)

        def lay(j, carry):
            at = pl.ds(pl.multiple_of(j * nb, nb), nb)
            lane = pl.ds(pl.multiple_of(j * 128, 128), 128)
            one = owner_hot[at, :]
            rank = jnp.sum(one * (prefix[at, 0:128] + carry), axis=0, keepdims=True)
            meta_b[:, lane] = jnp.where(iota((128, 128), 0).astype(F32) == rank, 1.0, 0.0).astype(BF16)
            v, t = voxel[pl.ds(j, 1), :], target[pl.ds(j, 1), :]
            k = link[pl.ds(j, 1), :]
            k1, rest = split2(k)
            k2, k3 = split2(rest)
            values = (
                (v >> 8).astype(F32), (v & 255).astype(F32), (t >> 8).astype(F32), (t & 255).astype(F32),
                k1, k2, k3,
            )
            for q, value in enumerate(values):
                meta_a[q * nb:(q + 1) * nb, lane] = (one * value).astype(BF16)
            return carry + prefix[at, 128:256]

        lax.fori_loop(0, groups, lay, jnp.zeros((nb, 128), F32))
        packet = dot(meta_a[...], meta_b[...], NT)
        part = [packet[q * nb:(q + 1) * nb] for q in range(PARTS)]
        cell_y[...], cell_z[...] = part[0], part[1]
        code = part[2] * 256.0 + part[3]
        k = part[4] + part[5] + part[6]
        link_p[...] = k
        for o in range(nb):
            meta_send[o, 0:1, :] = k[o:o + 1]
            meta_send[o, 1:2, :] = code[o:o + 1]

        def send(i, _):
            to = lax.rem(brick + i, nb)
            pltpu.make_async_remote_copy(
                src_ref=meta_send.at[to], dst_ref=meta_recv.at[dom * nb + brick],
                send_sem=meta_ssem, recv_sem=meta_rsem, device_id=(last, to, slab), device_id_type=MESH,
            ).start()
            return 0

        lax.fori_loop(0, nb, send, 0)

    zrow = iota((COLS, 128), 0).astype(F32)
    yrow = iota((ROWS, 128), 0).astype(F32)

    def hot_columns(z):
        return jnp.where(zrow == z, 1.0, 0.0).astype(BF16)

    def spread(value, y):
        a, b = split2(value)
        there = yrow == y
        return jnp.concatenate([jnp.where(there, a, 0.0), jnp.where(there, b, 0.0)], axis=0).astype(BF16)

    def total(x):
        return x[0:ROWS] + x[ROWS:2 * ROWS]

    def scatter(rows, group, row_of, build):
        def step(g, acc):
            parts, hots = [], []
            for j in range(group):
                value, y, z = row_of(g * group + j)
                parts.append(spread(value, y))
                if build:
                    hots.append(hot_columns(z))
            lane = pl.ds(pl.multiple_of(g * group * 128, 128), group * 128)
            if build:
                columns = jnp.concatenate(hots, axis=1)
                hot[:, lane] = columns
            else:
                columns = hot[:, lane]
            return acc + dot(jnp.concatenate(parts, axis=1), columns, NT)

        return total(lax.fori_loop(0, rows // group, step, jnp.zeros((2 * ROWS, COLS), F32)))

    def sheet_parts(x):
        return jnp.concatenate(split2(x), axis=0).astype(BF16)

    def gather(sheet, g, group, y_of):
        lane = pl.ds(pl.multiple_of(g * group * 128, 128), group * 128)
        got = total(dot(sheet, hot[:, lane], NN))
        return [
            jnp.sum(jnp.where(yrow == y_of(g * group + j), got[:, j * 128:(j + 1) * 128], 0.0), axis=0, keepdims=True)
            for j in range(group)
        ]

    group_p, group_l = math.gcd(8, nb), math.gcd(8, rows_in)

    @pl.when(jnp.logical_not(solid))
    def _():
        def packet_row(i):
            one = pl.ds(i, 1)
            return link_p[one, :], cell_y[one, :], cell_z[one, :]

        hsum[...] = scatter(nb, group_p, packet_row, True)

    for copy in a_copies:
        copy.wait()
    zr = jnp.concatenate([zst[0], jnp.where(row8n < W, dst8[0] * more_b, dst8[2] * less_b)], axis=0)
    zl = jnp.concatenate([zst[1], jnp.where(row8n < W, dst8[1] * more_b, dst8[3] * less_b)], axis=0)
    lane24 = iota((XR, 128), 1)
    for l in range(LAYERS):
        first_u, last_u = yst[0, l], yst[1, l]
        first_c, last_c = yst[0, LAYERS + l // 2], yst[1, LAYERS + l // 2]
        if l % 2:
            first_c = pltpu.roll(first_c, W, 0)
        else:
            last_c = pltpu.roll(last_c, W, 0)
        pairs = (
            (ua, first_u, pltpu.roll(last_u, W, 0)),
            (rx, pltpu.roll(first_u, W, 0), last_u),
            (cx, first_c, last_c),
        )
        for a, (x, after, prior) in enumerate(pairs):
            x[l, ROWS:XR, 0:COLS] = jnp.where(row8 < W, after * more_b, prior * less_b)
            g = (l * 3 + a) * W
            right = pltpu.roll(zr, 128 - g, 1) if g else zr
            left = pltpu.roll(zl, 128 - W - 64 - g, 1)
            x[l, :, COLS:XC] = sides(right, left, lane24)

    def sweep(x, y, source):
        for l in range(LAYERS):
            u = x[l]
            left = pltpu.roll(u, 1, 1)
            around = pltpu.roll(u, 1, 0) + pltpu.roll(u, XR - 1, 0) + left + pltpu.roll(u, XC - 1, 1)
            if l > 0:
                around = around + x[l - 1]
            if l < LAYERS - 1:
                around = around + x[l + 1]
            new = u + rx[l] * (around - 6.0 * u) - cx[l] * (u - left)
            if source and l == 0:
                new = new + (sx[0] - gx[0] * u)
            y[l] = new

    def phase(source):
        for repeat in range(SWEEPS // 2):
            sweep(ua, ub, source)
            sweep(ub, ua, source)

    phase(False)

    @pl.when(jnp.logical_not(solid))
    def _():
        sheet = sheet_parts(ua[0, 0:ROWS, 0:COLS])

        def step(g, _):
            rows = gather(sheet, g, group_p, lambda i: cell_y[pl.ds(i, 1), :])
            for j in range(group_p):
                i = g * group_p + j
                q_send[i] = rows[j] * link_p[pl.ds(i, 1), :]
            return 0

        lax.fori_loop(0, nb // group_p, step, 0)

        def send(i, _):
            to = lax.rem(brick + i, nb)
            pltpu.make_async_remote_copy(
                src_ref=q_send.at[to], dst_ref=q_recv.at[dom * nb + brick],
                send_sem=q_ssem, recv_sem=q_rsem, device_id=(last, to, slab), device_id_type=MESH,
            ).start()
            return 0

        lax.fori_loop(0, nb, send, 0)

    for copy in u_copies:
        copy.start()

    def whole(ref, ssem, rsem):
        return pltpu.make_async_remote_copy(
            src_ref=ref, dst_ref=ref, send_sem=ssem, recv_sem=rsem,
            device_id=neighbour(STEPS[0]), device_id_type=MESH,
        )

    def target_row(i, value):
        code = meta_recv[i, 1:2, :]
        y = jnp.floor(code * (1.0 / 256.0))
        return value, y, code - 256.0 * y

    @pl.when(solid)
    def _():
        for copy in slots:
            copy.wait()
        whole(meta_recv, meta_ssem, meta_rsem).wait_recv()
        gx[0, 0:ROWS, 0:COLS] = scatter(rows_in, group_l, lambda i: target_row(i, meta_recv[i, 0:1, :]), True)
        for copy in g_copies:
            copy.start()

    for copy in u_copies:
        copy.wait()
    unpack(ua, uy, uz, udg, LAYERS)

    @pl.when(solid)
    def _():
        for copy in g_copies:
            copy.wait()
        unpack(gx, gy, gz, gdg, 1)
        g = gx[0]
        inverse = 1.0 / (1.0 + g)
        gx[0] = g * inverse
        whole(q_recv, q_ssem, q_rsem).wait_recv()
        sx[0, 0:ROWS, 0:COLS] = scatter(rows_in, group_l, lambda i: target_row(i, q_recv[i]), False)
        for copy in s_copies:
            copy.start()
        for copy in s_copies:
            copy.wait()
        unpack(sx, sy, sz, sdg, 1)
        sx[0] = sx[0] * inverse
        phase(True)
        sheet = sheet_parts(ua[0, 0:ROWS, 0:COLS])

        def step(g, _):
            rows = gather(sheet, g, group_l, lambda i: target_row(i, None)[1])
            for j in range(group_l):
                i = g * group_l + j
                ans_send[i] = rows[j]
                pltpu.make_async_remote_copy(
                    src_ref=ans_send.at[i], dst_ref=wall_recv.at[brick],
                    send_sem=ans_ssem, recv_sem=ans_rsem,
                    device_id=(lax.div(i, nb), lax.rem(i, nb), slab), device_id_type=MESH,
                ).start()
            return 0

        lax.fori_loop(0, rows_in // group_l, step, 0)
        whole(ans_send, ans_ssem, ans_rsem).wait_send()

    @pl.when(jnp.logical_not(solid))
    def _():
        phase(False)
        whole(meta_send, meta_ssem, meta_rsem).wait_send()
        whole(q_send, q_ssem, q_rsem).wait_send()
        whole(wall_recv, ans_ssem, ans_rsem).wait_recv()

        def packet_row(i):
            one = pl.ds(i, 1)
            return link_p[one, :] * wall_recv[i], cell_y[one, :], None

        q = scatter(nb, group_p, packet_row, False)
        h = hsum[...]
        u = ua[0, 0:ROWS, 0:COLS]
        ua[0, 0:ROWS, 0:COLS] = u + (q - h * u) / (1.0 + h)

    done = pltpu.make_async_copy(ua.at[own], out, out_sem)
    done.start()
    done.wait()


def body(nd, nb, ns, heat, ratio, courant, voxel, owner, target, link, tally):
    groups = voxel.size // 128
    slots = [x.reshape(groups, 128) for x in (voxel, owner, target, link)]
    rows_in = (nd - 1) * nb
    most = max(rows_in, nb)
    vm = pltpu.VMEM
    sem = pltpu.SemaphoreType.DMA

    def stage(layers):
        return [vm((2, layers, 8, COLS), F32), vm((2, layers, ROWS, 128), F32), vm((4, layers, 8, 128), F32)]

    field = vm((LAYERS, XR, XC), F32)
    scratch = (
        [field] * 4 + [vm((1, XR, XC), F32)] * 2
        + [vm((groups, 128), I32)] * 3 + [vm((groups, 128), F32)]
        + [vm((2, LAYERS + 2, 8, COLS), F32), vm((ROWS, 128), F32)]
        + [vm((2, LAYERS + 2, 8, COLS), F32), vm((2, ROWS, 128), F32), vm((4, 8, 128), F32)]
        + stage(LAYERS) + stage(1) + stage(1)
        + [vm((COLS, most * CAP), BF16), vm((groups * nb, 128), F32), vm((groups * nb, 256), F32)]
        + [vm((PARTS * nb, groups * 128), BF16), vm((128, groups * 128), BF16)]
        + [vm((nb, CAP), F32)] * 3 + [vm((nb, CAP), F32)] * 2 + [vm((ROWS, COLS), F32)]
        + [vm((nb, 2, CAP), F32), vm((nb, 1, CAP), F32), vm((rows_in, 2, CAP), F32), vm((rows_in, 1, CAP), F32)]
        + [vm((rows_in, 1, CAP), F32), vm((nb, 1, CAP), F32)]
        + [sem((3,)), sem((4,)), sem]
        + [sem((8,))] * 8
        + [sem] * 6
    )
    hbm = pl.BlockSpec(memory_space=pl.ANY)
    return pl.pallas_call(
        functools.partial(kernel, nd, nb, ns),
        out_shape=jax.ShapeDtypeStruct(heat.shape, F32),
        in_specs=[hbm] * 7 + [pl.BlockSpec(memory_space=pltpu.SMEM)],
        out_specs=hbm,
        scratch_shapes=scratch,
        compiler_params=pltpu.CompilerParams(
            collective_id=0, has_side_effects=True, vmem_limit_bytes=40 * 1024 * 1024
        ),
    )(heat, ratio, courant, *slots, tally.reshape(1))


def solution(mesh):
    nd, nb, ns = (mesh.shape[a] for a in ("dom", "brick", "slab"))
    where = P("dom", "brick", "slab")
    return jax.shard_map(
        functools.partial(body, nd, nb, ns),
        mesh=mesh,
        in_specs=(where,) * 8,
        out_specs=where,
        check_vma=False,
    )
```

time: 647 us -> 64.4 us (0.10)
  other arithmetic: 222 us -> 0 us
  starting transfers between devices: 128 us -> 0 us
  local copies, waits for them, and re-layouts: 128 us -> 5.27 us
  waiting for transfers between devices: 115 us -> 0 us
  Pallas kernels: 0 us -> 58 us
  blocking collectives: 37.1 us -> 0 us
  between operations: 15.1 us -> 0.68 us
    scatter-add x5 -> x0, other arithmetic: 217 us -> none  [the longest x1 96.9 us: body(): jnp.zeros((sheet_lines * sheet_columns,), jnp.float32).at[land_cell]]
    gather x3 -> x0, local copies, waits for them, and re-layouts: 114 us -> none  [the longest x1 90.5 us: body(): answer = liner_current[land_cell].reshape(region_total, bricks, slot_cap)]
    ppermute x32 -> x0, starting transfers between devices: 114 us -> none  [the longest x16 93 us: extended(): lax.ppermute(tail, axis, [(i, (i + 1) % count) for i in range(ends)])]
    ppermute x32 -> x0, waiting for transfers between devices: 59.4 us -> none  [the longest x16 59.3 us: extended(): lax.ppermute(head, axis, [((i + 1) % count, i) for i in range(ends)])]
    pallas_call x0 -> x1, Pallas kernels: none -> 58 us  [body(): pl.pallas_call(functools.partial(kernel, nd, nb, ns), out_shape=jax.Shape...]
    psum x1 -> x0, waiting for transfers between devices: 53.4 us -> none  [spread(): return lax.psum(block, axis)]
    all_to_all x1 -> x0, blocking collectives: 20.4 us -> none  [body(): lax.all_to_all(answer, 'brick', split_axis=1, concat_axis=1, tiled=True)]
    all_gather x1 -> x0, blocking collectives: 16.7 us -> none  [body(): grouped = lax.all_gather(packet[None], 'dom', axis=0, tiled=True)]
  transfers between devices with their start and end apart: 34 -> 0, of which waited for: 17 -> 0; matrix products, arithmetic and copies ran while one was open for 4% -> 0% of each run, Pallas kernels for 0% -> 0%
where the time goes in v1:
time: 64.4 us; the launch traced here: 63.9 us
  Pallas kernels  58 us (90%)
  local copies, waits for them, and re-layouts  5.27 us (8%)
  between operations  0.68 us (1%)
    pallas_call x1, Pallas kernels, body(): pl.pallas_call(functools.partial(kernel, nd, nb, ns), out_shape=jax.Shape...  58 us
    unnamed x15, local copies, waits for them, and re-layouts  5.27 us

profile of v1, /device:TPU:1, one launch (start us, length us, event | category | flops | bytes accessed | tf_op | source)
XLA Modules:
  0.0 63.9 jit_solution(10980595967754236162)
XLA Ops:
  0.0 0.0 copy-start.3
  0.7 0.0 copy-done.3
  0.7 0.0 copy-start
  0.7 0.8 %copy-done = f32[4,16,256]{2,1,0:T(8,128)S(1)} copy-done((f32[4,16,256]{2,1,0:T(8,128)S(1)}, f32[4,16,256]{2,1,0:T(8,128)}, u32[]{:S(2)}) %copy-start) | copy-done | bytes 65560
  1.5 0.0 copy-start.1
  1.5 0.8 %copy-done.1 = f32[4,16,256]{2,1,0:T(8,128)S(1)} copy-done((f32[4,16,256]{2,1,0:T(8,128)S(1)}, f32[4,16,256]{2,1,0:T(8,128)}, u32[]{:S(2)}) %copy-start.1) | copy-done | bytes 65560
  2.4 0.0 copy-start.2
  2.4 0.8 %copy-done.2 = f32[4,16,256]{2,1,0:T(8,128)S(1)} copy-done((f32[4,16,256]{2,1,0:T(8,128)S(1)}, f32[4,16,256]{2,1,0:T(8,128)}, u32[]{:S(2)}) %copy-start.2) | copy-done | bytes 65560
  3.2 0.0 copy-start.4
  3.2 0.7 %copy-done.4 = s32[1,1,1,2048,1]{3,4,2,1,0:T(1,128)S(1)} copy-done((s32[1,1,1,2048,1]{3,4,2,1,0:T(1,128)S(1)}, s32[1,1,1,2048,1]{3,4,2,1,0:T(1,128)}, u32[]{:S(2)}) %copy-start.4) | copy-done | bytes 8216
  3.9 0.0 copy-start.5
  3.9 0.7 %copy-done.5 = s32[1,1,1,2048]{3,2,1,0:T(1,128)S(1)} copy-done((s32[1,1,1,2048]{3,2,1,0:T(1,128)S(1)}, s32[1,1,1,2048]{3,2,1,0:T(1,128)}, u32[]{:S(2)}) %copy-start.5) | copy-done | bytes 8216
  4.6 0.0 copy-start.6
  4.6 0.7 %copy-done.6 = f32[1,1,1,2048]{3,2,1,0:T(1,128)S(1)} copy-done((f32[1,1,1,2048]{3,2,1,0:T(1,128)S(1)}, f32[1,1,1,2048]{3,2,1,0:T(1,128)}, u32[]{:S(2)}) %copy-start.6) | copy-done | bytes 8216
  5.3 58.0 %shard_map.82 = f32[4,16,256]{2,1,0:T(8,128)S(1)} custom-call(f32[4,16,256]{2,1,0:T(8,128)S(1)} %copy-done, f32[4,16,256]{2,1,0:T(8,128)S(1)} %copy-done.1, f32[4,16,256]{2,1,0:T(8,128)S(1)} %copy-done.2, s32[16,128]{1,0:T(8,128)S(1)} %bitcast.6, s32[16,128]{1,0:T(8,128)S(1)} %bitcast.7, s32[16,128]{1,0:T(8,128)S(1)} %bitcast.8, f32[16,128]{1,0:T(8,128)S(1)} %bitcast.9, ...), custom_call_target="tpu_custom_call" | custom-call | tf_op jit(solution)/shard_map/pallas_call | solution.py:470
  63.3 0.6 copy.11
Async XLA Ops:
  0.0 0.7 %copy-start.3 = (s32[1,1,1,2048]{3,2,1,0:T(1,128)S(1)}, s32[1,1,1,2048]{3,2,1,0:T(1,128)}, u32[]{:S(2)}) copy-start(s32[1,1,1,2048]{3,2,1,0:T(1,128)} %param.11) | copy-start | bytes 24580
  0.7 0.8 %copy-start = (f32[4,16,256]{2,1,0:T(8,128)S(1)}, f32[4,16,256]{2,1,0:T(8,128)}, u32[]{:S(2)}) copy-start(f32[4,16,256]{2,1,0:T(8,128)} %heat.1) | copy-start | bytes 196612
  1.5 0.8 %copy-start.1 = (f32[4,16,256]{2,1,0:T(8,128)S(1)}, f32[4,16,256]{2,1,0:T(8,128)}, u32[]{:S(2)}) copy-start(f32[4,16,256]{2,1,0:T(8,128)} %ratio.1) | copy-start | bytes 196612
  2.4 0.8 %copy-start.2 = (f32[4,16,256]{2,1,0:T(8,128)S(1)}, f32[4,16,256]{2,1,0:T(8,128)}, u32[]{:S(2)}) copy-start(f32[4,16,256]{2,1,0:T(8,128)} %courant.1) | copy-start | bytes 196612
  3.2 0.7 %copy-start.4 = (s32[1,1,1,2048,1]{3,4,2,1,0:T(1,128)S(1)}, s32[1,1,1,2048,1]{3,4,2,1,0:T(1,128)}, u32[]{:S(2)}) copy-start(s32[1,1,1,2048,1]{3,4,2,1,0:T(1,128)} %param.12) | copy-start | bytes 24580
  3.9 0.7 %copy-start.5 = (s32[1,1,1,2048]{3,2,1,0:T(1,128)S(1)}, s32[1,1,1,2048]{3,2,1,0:T(1,128)}, u32[]{:S(2)}) copy-start(s32[1,1,1,2048]{3,2,1,0:T(1,128)} %param.13) | copy-start | bytes 24580
  4.6 0.7 %copy-start.6 = (f32[1,1,1,2048]{3,2,1,0:T(1,128)S(1)}, f32[1,1,1,2048]{3,2,1,0:T(1,128)}, u32[]{:S(2)}) copy-start(f32[1,1,1,2048]{3,2,1,0:T(1,128)} %param.14) | copy-start | bytes 24580

commit v2 on v1

--- a/solution.py
+++ b/solution.py
@@ -11,6 +11,7 @@
 SWEEPS = 4
 W = 4
 CAP = 128
+VMEM_BYTES = 60 * 1024 * 1024
 LAYERS, ROWS, COLS = 4, 16, 256
 XR, XC = ROWS + 8, COLS + 128
 PARTS = 7
@@ -43,7 +44,7 @@
     ysend, zsend, yst, zst, dst8,
     uy, uz, udg, gy, gz, gdg, sy, sz, sdg,
     hot, owner_hot, prefix, meta_a, meta_b,
-    cell_y, cell_z, link_p, q_rows, wall_rows, hsum,
+    cell_y, cell_z, link_p, hsum,
     meta_send, q_send, meta_recv, q_recv, ans_send, wall_recv,
     in_sem, slot_sem, out_sem,
     a_send, a_recv, u_send, u_recv, g_send, g_recv, s_send, s_recv,
@@ -53,6 +54,16 @@
     last = nd - 1
     solid = dom == last
     rows_in = last * nb
+    wide = math.gcd(4, nb)
+    lines = nb // wide
+    deep = last * wide
+    my_line, my_place = lax.div(brick, wide), lax.rem(brick, wide)
+    my_row = my_line * deep + dom * wide + my_place
+
+    def far_first(t):
+        k = lax.div(t + 1, 2)
+        away = lines // 2 + jnp.where(lax.rem(t, 2) == 0, k, -k)
+        return lax.rem(my_line + away + lines, lines)
 
     own = (slice(None), pl.ds(0, ROWS), pl.ds(0, COLS))
     fields = [
@@ -63,18 +74,30 @@
         pltpu.make_async_copy(h, v, slot_sem.at[i])
         for i, (h, v) in enumerate(((owner_h, owner), (voxel_h, voxel), (target_h, target), (link_h, link)))
     ]
+
+    def neighbour(step):
+        db, dz = step
+        return (dom, lax.rem(brick + db + nb, nb), lax.rem(slab + dz + ns, ns))
+
+    def exists(step):
+        db, dz = step
+        b, z = brick + db, slab + dz
+        return (b >= 0) & (b < nb) & (z >= 0) & (z < ns)
+
+    def on(step, act):
+        pl.when(exists(step))(act)
+
+    barrier = pltpu.get_barrier_semaphore()
+    for step in STEPS:
+
+        @functools.partial(on, step)
+        def _():
+            pl.semaphore_signal(barrier, inc=1, device_id=neighbour(step), device_id_type=MESH)
+
     for copy in fields:
         copy.start()
     for copy in slots:
         copy.start()
-
-    def neighbour(step):
-        db, dz = step
-        return (dom, lax.rem(brick + db + nb, nb), lax.rem(slab + dz + ns, ns))
-
-    barrier = pltpu.get_barrier_semaphore()
-    for step in STEPS:
-        pl.semaphore_signal(barrier, inc=1, device_id=neighbour(step), device_id_type=MESH)
 
     @pl.when(solid)
     def _():
@@ -96,10 +119,10 @@
         lax.fori_loop(0, nb, greet, 0)
 
     gas = jnp.where(solid, 0.0, 1.0).astype(F32)
-    more_b = jnp.where(brick < nb - 1, 1.0, 0.0).astype(F32)
-    less_b = jnp.where(brick > 0, 1.0, 0.0).astype(F32)
-    more_z = jnp.where(slab < ns - 1, 1.0, 0.0).astype(F32)
-    less_z = jnp.where(slab > 0, 1.0, 0.0).astype(F32)
+    rows_end = jnp.where(brick < nb - 1, W, 0)
+    rows_from = jnp.where(brick > 0, 8 - W, 8)
+    lanes_end = jnp.where(slab < ns - 1, W, 0)
+    lanes_from = jnp.where(slab > 0, 128 - W, 128)
 
     for copy in fields:
         copy.wait()
@@ -122,8 +145,8 @@
             packed = jnp.where((lane16 >= 64 + g) & (lane16 < 64 + g + W), tail, packed)
     zsend[...] = packed
 
-    count = jnp.where(solid, len(STEPS) + rows_in, len(STEPS) + nb)
-    pl.semaphore_wait(barrier, count)
+    beside = sum(jnp.where(exists(step), 1, 0) for step in STEPS)
+    pl.semaphore_wait(barrier, beside + jnp.where(solid, rows_in, nb))
 
     def halo_copies(sources, landings, ssem, rsem):
         return [
@@ -134,14 +157,22 @@
             for m, step in enumerate(STEPS)
         ]
 
+    def begin(copies):
+        for m in reversed(range(len(STEPS))):
+            on(STEPS[m], copies[m].start)
+
+    def finish(copies):
+        for m, (db, dz) in enumerate(STEPS):
+            on((db, dz), copies[m].wait_send)
+            on((-db, -dz), copies[m].wait_recv)
+
     low, high = zsend.at[pl.ds(0, 8)], zsend.at[pl.ds(ROWS - 8, 8)]
     a_copies = halo_copies(
         [ysend.at[0], ysend.at[1], zsend, zsend, low, low, high, high],
         [yst.at[0], yst.at[1], zst.at[0], zst.at[1]] + [dst8.at[i] for i in range(4)],
         a_send, a_recv,
     )
-    for copy in a_copies:
-        copy.start()
+    begin(a_copies)
 
     def sheet_copies(x, y, z, d, ssem, rsem):
         def part(r0, rn, c0, cn):
@@ -167,14 +198,17 @@
     lane8 = iota((8, 128), 1)
 
     def sides(right, left, lanes):
-        return jnp.where(lanes < W, right * more_z, jnp.where(lanes >= 128 - W, left * less_z, 0.0))
+        return jnp.where(lanes < lanes_end, right, jnp.where(lanes >= lanes_from, left, 0.0))
+
+    def ends(after, prior, rows):
+        return jnp.where(rows < rows_end, after, jnp.where(rows >= rows_from, prior, 0.0))
 
     def unpack(x, y, z, d, layers):
         for l in range(layers):
-            x[l, ROWS:XR, 0:COLS] = jnp.where(row8 < W, y[0, l] * more_b, y[1, l] * less_b)
+            x[l, ROWS:XR, 0:COLS] = ends(y[0, l], y[1, l], row8)
             x[l, 0:ROWS, COLS:XC] = sides(z[0, l], z[1, l], lane16)
-            right = jnp.where(row8n < W, d[0, l] * more_b, d[2, l] * less_b)
-            left = jnp.where(row8n < W, d[1, l] * more_b, d[3, l] * less_b)
+            right = ends(d[0, l], d[2, l], row8n)
+            left = ends(d[1, l], d[3, l], row8n)
             x[l, ROWS:XR, COLS:XC] = sides(right, left, lane8)
 
     @pl.when(jnp.logical_not(solid))
@@ -227,10 +261,10 @@
             meta_send[o, 1:2, :] = code[o:o + 1]
 
         def send(i, _):
-            to = lax.rem(brick + i, nb)
+            to = far_first(lax.div(i, wide)) * wide + lax.rem(i, wide)
             pltpu.make_async_remote_copy(
-                src_ref=meta_send.at[to], dst_ref=meta_recv.at[dom * nb + brick],
-                send_sem=meta_ssem, recv_sem=meta_rsem, device_id=(last, to, slab), device_id_type=MESH,
+                src_ref=meta_send.at[to], dst_ref=meta_recv.at[my_row],
+                send_sem=meta_ssem, recv_sem=meta_rsem.at[my_line], device_id=(last, to, slab), device_id_type=MESH,
             ).start()
             return 0
 
@@ -250,36 +284,39 @@
     def total(x):
         return x[0:ROWS] + x[ROWS:2 * ROWS]
 
-    def scatter(rows, group, row_of, build):
-        def step(g, acc):
-            parts, hots = [], []
-            for j in range(group):
-                value, y, z = row_of(g * group + j)
-                parts.append(spread(value, y))
+    def scatter(steps, group, blocks_of, row_of, build):
+        def step(t, acc):
+            blocks = blocks_of(t)
+            for first in blocks:
+                parts, hots = [], []
+                for j in range(group):
+                    value, y, z = row_of(first + j)
+                    parts.append(spread(value, y))
+                    if build:
+                        hots.append(hot_columns(z))
+                lane = pl.ds(pl.multiple_of(first * 128, 128), group * 128)
                 if build:
-                    hots.append(hot_columns(z))
-            lane = pl.ds(pl.multiple_of(g * group * 128, 128), group * 128)
-            if build:
-                columns = jnp.concatenate(hots, axis=1)
-                hot[:, lane] = columns
-            else:
-                columns = hot[:, lane]
-            return acc + dot(jnp.concatenate(parts, axis=1), columns, NT)
-
-        return total(lax.fori_loop(0, rows // group, step, jnp.zeros((2 * ROWS, COLS), F32)))
+                    columns = jnp.concatenate(hots, axis=1)
+                    hot[:, lane] = columns
+                else:
+                    columns = hot[:, lane]
+                acc = acc + dot(jnp.concatenate(parts, axis=1), columns, NT)
+            return acc
+
+        return total(lax.fori_loop(0, steps, step, jnp.zeros((2 * ROWS, COLS), F32)))
 
     def sheet_parts(x):
         return jnp.concatenate(split2(x), axis=0).astype(BF16)
 
-    def gather(sheet, g, group, y_of):
-        lane = pl.ds(pl.multiple_of(g * group * 128, 128), group * 128)
+    def gather(sheet, first, group, y_of, put):
+        lane = pl.ds(pl.multiple_of(first * 128, 128), group * 128)
         got = total(dot(sheet, hot[:, lane], NN))
-        return [
-            jnp.sum(jnp.where(yrow == y_of(g * group + j), got[:, j * 128:(j + 1) * 128], 0.0), axis=0, keepdims=True)
-            for j in range(group)
-        ]
-
-    group_p, group_l = math.gcd(8, nb), math.gcd(8, rows_in)
+        for j in range(group):
+            here = jnp.where(yrow == y_of(first + j), got[:, j * 128:(j + 1) * 128], 0.0)
+            put(first + j, jnp.sum(here, axis=0, keepdims=True))
+
+    pair = math.gcd(2, lines)
+    group_p = math.gcd(8, nb)
 
     @pl.when(jnp.logical_not(solid))
     def _():
@@ -287,12 +324,11 @@
             one = pl.ds(i, 1)
             return link_p[one, :], cell_y[one, :], cell_z[one, :]
 
-        hsum[...] = scatter(nb, group_p, packet_row, True)
-
-    for copy in a_copies:
-        copy.wait()
-    zr = jnp.concatenate([zst[0], jnp.where(row8n < W, dst8[0] * more_b, dst8[2] * less_b)], axis=0)
-    zl = jnp.concatenate([zst[1], jnp.where(row8n < W, dst8[1] * more_b, dst8[3] * less_b)], axis=0)
+        hsum[...] = scatter(nb // group_p, group_p, lambda t: [t * group_p], packet_row, True)
+
+    finish(a_copies)
+    zr = jnp.concatenate([zst[0], ends(dst8[0], dst8[2], row8n)], axis=0)
+    zl = jnp.concatenate([zst[1], ends(dst8[1], dst8[3], row8n)], axis=0)
     lane24 = iota((XR, 128), 1)
     for l in range(LAYERS):
         first_u, last_u = yst[0, l], yst[1, l]
@@ -307,7 +343,7 @@
             (cx, first_c, last_c),
         )
         for a, (x, after, prior) in enumerate(pairs):
-            x[l, ROWS:XR, 0:COLS] = jnp.where(row8 < W, after * more_b, prior * less_b)
+            x[l, ROWS:XR, 0:COLS] = ends(after, prior, row8)
             g = (l * 3 + a) * W
             right = pltpu.roll(zr, 128 - g, 1) if g else zr
             left = pltpu.roll(zl, 128 - W - 64 - g, 1)
@@ -338,27 +374,25 @@
     def _():
         sheet = sheet_parts(ua[0, 0:ROWS, 0:COLS])
 
-        def step(g, _):
-            rows = gather(sheet, g, group_p, lambda i: cell_y[pl.ds(i, 1), :])
-            for j in range(group_p):
-                i = g * group_p + j
-                q_send[i] = rows[j] * link_p[pl.ds(i, 1), :]
+        def put(i, row):
+            q_send[i] = row * link_p[pl.ds(i, 1), :]
+
+        def step(t, _):
+            firsts = [far_first(t * pair + a) * wide for a in range(pair)]
+            for first in firsts:
+                gather(sheet, first, wide, lambda i: cell_y[pl.ds(i, 1), :], put)
+            for first in firsts:
+                for j in range(wide):
+                    pltpu.make_async_remote_copy(
+                        src_ref=q_send.at[first + j], dst_ref=q_recv.at[my_row],
+                        send_sem=q_ssem, recv_sem=q_rsem.at[my_line],
+                        device_id=(last, first + j, slab), device_id_type=MESH,
+                    ).start()
             return 0
 
-        lax.fori_loop(0, nb // group_p, step, 0)
-
-        def send(i, _):
-            to = lax.rem(brick + i, nb)
-            pltpu.make_async_remote_copy(
-                src_ref=q_send.at[to], dst_ref=q_recv.at[dom * nb + brick],
-                send_sem=q_ssem, recv_sem=q_rsem, device_id=(last, to, slab), device_id_type=MESH,
-            ).start()
-            return 0
-
-        lax.fori_loop(0, nb, send, 0)
-
-    for copy in u_copies:
-        copy.start()
+        lax.fori_loop(0, lines // pair, step, 0)
+
+    begin(u_copies)
 
     def whole(ref, ssem, rsem):
         return pltpu.make_async_remote_copy(
@@ -366,6 +400,11 @@
             device_id=neighbour(STEPS[0]), device_id_type=MESH,
         )
 
+    def line_in(t, ref, ssem, rsem):
+        line = lines - 1 - t
+        whole(ref.at[pl.ds(line * deep, deep)], ssem, rsem.at[line]).wait_recv()
+        return [line * deep]
+
     def target_row(i, value):
         code = meta_recv[i, 1:2, :]
         y = jnp.floor(code * (1.0 / 256.0))
@@ -375,61 +414,71 @@
     def _():
         for copy in slots:
             copy.wait()
-        whole(meta_recv, meta_ssem, meta_rsem).wait_recv()
-        gx[0, 0:ROWS, 0:COLS] = scatter(rows_in, group_l, lambda i: target_row(i, meta_recv[i, 0:1, :]), True)
-        for copy in g_copies:
-            copy.start()
-
-    for copy in u_copies:
-        copy.wait()
+        gx[0, 0:ROWS, 0:COLS] = scatter(
+            lines, deep, lambda t: line_in(t, meta_recv, meta_ssem, meta_rsem),
+            lambda i: target_row(i, meta_recv[i, 0:1, :]), True,
+        )
+        begin(g_copies)
+
+    finish(u_copies)
     unpack(ua, uy, uz, udg, LAYERS)
 
     @pl.when(solid)
     def _():
-        for copy in g_copies:
-            copy.wait()
+        finish(g_copies)
         unpack(gx, gy, gz, gdg, 1)
         g = gx[0]
         inverse = 1.0 / (1.0 + g)
         gx[0] = g * inverse
-        whole(q_recv, q_ssem, q_rsem).wait_recv()
-        sx[0, 0:ROWS, 0:COLS] = scatter(rows_in, group_l, lambda i: target_row(i, q_recv[i]), False)
-        for copy in s_copies:
-            copy.start()
-        for copy in s_copies:
-            copy.wait()
+        sx[0, 0:ROWS, 0:COLS] = scatter(
+            lines, deep, lambda t: line_in(t, q_recv, q_ssem, q_rsem), lambda i: target_row(i, q_recv[i]), False
+        )
+        begin(s_copies)
+        finish(s_copies)
         unpack(sx, sy, sz, sdg, 1)
         sx[0] = sx[0] * inverse
         phase(True)
         sheet = sheet_parts(ua[0, 0:ROWS, 0:COLS])
 
-        def step(g, _):
-            rows = gather(sheet, g, group_l, lambda i: target_row(i, None)[1])
-            for j in range(group_l):
-                i = g * group_l + j
-                ans_send[i] = rows[j]
-                pltpu.make_async_remote_copy(
-                    src_ref=ans_send.at[i], dst_ref=wall_recv.at[brick],
-                    send_sem=ans_ssem, recv_sem=ans_rsem,
-                    device_id=(lax.div(i, nb), lax.rem(i, nb), slab), device_id_type=MESH,
-                ).start()
+        def put(i, row):
+            ans_send[i] = row
+
+        def step(t, _):
+            to_lines = [far_first(t * pair + a) for a in range(pair)]
+            for line in to_lines:
+                gather(sheet, line * deep, deep, lambda i: target_row(i, None)[1], put)
+            for line in to_lines:
+                for j in range(deep):
+                    pltpu.make_async_remote_copy(
+                        src_ref=ans_send.at[line * deep + j], dst_ref=wall_recv.at[brick],
+                        send_sem=ans_ssem, recv_sem=ans_rsem.at[my_line],
+                        device_id=(j // wide, line * wide + j % wide, slab), device_id_type=MESH,
+                    ).start()
             return 0
 
-        lax.fori_loop(0, rows_in // group_l, step, 0)
-        whole(ans_send, ans_ssem, ans_rsem).wait_send()
+        lax.fori_loop(0, lines // pair, step, 0)
+        whole(ans_send, ans_ssem, ans_rsem.at[0]).wait_send()
 
     @pl.when(jnp.logical_not(solid))
     def _():
         phase(False)
-        whole(meta_send, meta_ssem, meta_rsem).wait_send()
-        whole(q_send, q_ssem, q_rsem).wait_send()
-        whole(wall_recv, ans_ssem, ans_rsem).wait_recv()
+        whole(meta_send, meta_ssem, meta_rsem.at[0]).wait_send()
+        whole(q_send, q_ssem, q_rsem.at[0]).wait_send()
 
         def packet_row(i):
             one = pl.ds(i, 1)
             return link_p[one, :] * wall_recv[i], cell_y[one, :], None
 
-        q = scatter(nb, group_p, packet_row, False)
+        def lines_in(t):
+            firsts = []
+            for a in range(pair):
+                line = far_first(lines - 1 - t * pair - a)
+                ref = wall_recv.at[pl.ds(line * wide, wide)]
+                whole(ref, ans_ssem, ans_rsem.at[line]).wait_recv()
+                firsts.append(line * wide)
+            return firsts
+
+        q = scatter(lines // pair, wide, lines_in, packet_row, False)
         h = hsum[...]
         u = ua[0, 0:ROWS, 0:COLS]
         ua[0, 0:ROWS, 0:COLS] = u + (q - h * u) / (1.0 + h)
@@ -444,6 +493,7 @@
     slots = [x.reshape(groups, 128) for x in (voxel, owner, target, link)]
     rows_in = (nd - 1) * nb
     most = max(rows_in, nb)
+    lines = nb // math.gcd(4, nb)
     vm = pltpu.VMEM
     sem = pltpu.SemaphoreType.DMA
 
@@ -459,12 +509,12 @@
         + stage(LAYERS) + stage(1) + stage(1)
         + [vm((COLS, most * CAP), BF16), vm((groups * nb, 128), F32), vm((groups * nb, 256), F32)]
         + [vm((PARTS * nb, groups * 128), BF16), vm((128, groups * 128), BF16)]
-        + [vm((nb, CAP), F32)] * 3 + [vm((nb, CAP), F32)] * 2 + [vm((ROWS, COLS), F32)]
+        + [vm((nb, CAP), F32)] * 3 + [vm((ROWS, COLS), F32)]
         + [vm((nb, 2, CAP), F32), vm((nb, 1, CAP), F32), vm((rows_in, 2, CAP), F32), vm((rows_in, 1, CAP), F32)]
         + [vm((rows_in, 1, CAP), F32), vm((nb, 1, CAP), F32)]
         + [sem((3,)), sem((4,)), sem]
         + [sem((8,))] * 8
-        + [sem] * 6
+        + [sem, sem((lines,))] * 3
     )
     hbm = pl.BlockSpec(memory_space=pl.ANY)
     return pl.pallas_call(
@@ -474,7 +524,7 @@
         out_specs=hbm,
         scratch_shapes=scratch,
         compiler_params=pltpu.CompilerParams(
-            collective_id=0, has_side_effects=True, vmem_limit_bytes=40 * 1024 * 1024
+            collective_id=0, has_side_effects=True, vmem_limit_bytes=VMEM_BYTES
         ),
     )(heat, ratio, courant, *slots, tally.reshape(1))
 

time: 64.4 us -> 48.8 us (0.76)
  Pallas kernels: 58 us -> 46 us
  local copies, waits for them, and re-layouts: 5.27 us -> 1.47 us
    pallas_call x1, Pallas kernels: 58 us -> 46 us  [body(): pl.pallas_call(functools.partial(kernel, nd, nb, ns), out_shape=jax.Shape...]
    unnamed x15 -> x1, local copies, waits for them, and re-layouts: 5.27 us -> 1.47 us
where the time goes in v2:
time: 48.8 us; the launch traced here: 48.2 us
  Pallas kernels  46 us (94%)
  local copies, waits for them, and re-layouts  1.47 us (3%)
  between operations  0.66 us (1%)
    pallas_call x1, Pallas kernels, body(): pl.pallas_call(functools.partial(kernel, nd, nb, ns), out_shape=jax.Shape...  46 us
    unnamed x1, local copies, waits for them, and re-layouts  1.47 us

profile of v2, /device:TPU:1, one launch (start us, length us, event | category | flops | bytes accessed | tf_op | source)
XLA Modules:
  0.0 48.2 jit_solution(14859146129163532031)
XLA Ops:
  0.7 46.0 %shard_map.82 = f32[4,16,256]{2,1,0:T(8,128)} custom-call(f32[4,16,256]{2,1,0:T(8,128)} %heat.1, f32[4,16,256]{2,1,0:T(8,128)} %ratio.1, f32[4,16,256]{2,1,0:T(8,128)} %courant.1, s32[16,128]{1,0:T(8,128)} %bitcast.6, s32[16,128]{1,0:T(8,128)} %bitcast.7, s32[16,128]{1,0:T(8,128)} %bitcast.8, f32[16,128]{1,0:T(8,128)} %bitcast.9, s32[1]{0:T(128)} %bitcast.5.tally), custom_call_target="tpu_custom_call" | custom-call | tf_op jit(solution)/shard_map/pallas_call | solution.py:520
  46.7 1.5 %copy.11 = f32[4,16,256]{2,1,0:T(8,128)} copy(f32[4,16,256]{2,1,0:T(8,128)} %shard_map.82) | data formatting | bytes 131072

commit v3 on v2

--- a/solution.py
+++ b/solution.py
@@ -37,10 +37,10 @@
 
 def kernel(
     nd, nb, ns,
-    heat, ratio, courant, voxel_h, owner_h, target_h, link_h, tally,
+    heat, ratio, courant, voxel_h, owner_h, target_h, link_h, tally_h,
     out,
     ua, ub, rx, cx, gx, sx,
-    voxel, owner, target, link,
+    voxel, owner, target, link, tally,
     ysend, zsend, yst, zst, dst8,
     uy, uz, udg, gy, gz, gdg, sy, sz, sdg,
     hot, owner_hot, prefix, meta_a, meta_b,
@@ -48,7 +48,7 @@
     meta_send, q_send, meta_recv, q_recv, ans_send, wall_recv,
     in_sem, slot_sem, out_sem,
     a_send, a_recv, u_send, u_recv, g_send, g_recv, s_send, s_recv,
-    meta_ssem, meta_rsem, q_ssem, q_rsem, ans_ssem, ans_rsem,
+    ready, meta_ssem, meta_rsem, q_ssem, q_rsem, ans_ssem, ans_rsem,
 ):
     dom, brick, slab = lax.axis_index("dom"), lax.axis_index("brick"), lax.axis_index("slab")
     last = nd - 1
@@ -72,7 +72,7 @@
     ]
     slots = [
         pltpu.make_async_copy(h, v, slot_sem.at[i])
-        for i, (h, v) in enumerate(((owner_h, owner), (voxel_h, voxel), (target_h, target), (link_h, link)))
+        for i, (h, v) in enumerate(((owner_h, owner), (voxel_h, voxel), (target_h, target), (link_h, link), (tally_h, tally)))
     ]
 
     def neighbour(step):
@@ -88,35 +88,34 @@
         pl.when(exists(step))(act)
 
     barrier = pltpu.get_barrier_semaphore()
+
+    def greet(*device):
+        pl.semaphore_signal(barrier, inc=1, device_id=device, device_id_type=MESH)
+
     for step in STEPS:
-
-        @functools.partial(on, step)
-        def _():
-            pl.semaphore_signal(barrier, inc=1, device_id=neighbour(step), device_id_type=MESH)
+        if step[1] >= 0:
+
+            @functools.partial(on, step)
+            def _():
+                greet(*neighbour(step))
+
+    @pl.when(solid)
+    def _():
+        def other(i, _):
+            greet(last, lax.rem(my_line + i, lines) * wide + my_place, slab)
+            return 0
+
+        lax.fori_loop(1, lines, other, 0)
+
+    @pl.when(jnp.logical_not(solid))
+    def _():
+        for j in range(wide):
+            greet(last, my_line * wide + j, slab)
 
     for copy in fields:
         copy.start()
     for copy in slots:
         copy.start()
-
-    @pl.when(solid)
-    def _():
-        def greet(i, _):
-            for d in range(last):
-                to = lax.rem(brick + i, nb)
-                pl.semaphore_signal(barrier, inc=1, device_id=(d, to, slab), device_id_type=MESH)
-            return 0
-
-        lax.fori_loop(0, nb, greet, 0)
-
-    @pl.when(jnp.logical_not(solid))
-    def _():
-        def greet(i, _):
-            to = lax.rem(brick + i, nb)
-            pl.semaphore_signal(barrier, inc=1, device_id=(last, to, slab), device_id_type=MESH)
-            return 0
-
-        lax.fori_loop(0, nb, greet, 0)
 
     gas = jnp.where(solid, 0.0, 1.0).astype(F32)
     rows_end = jnp.where(brick < nb - 1, W, 0)
@@ -145,8 +144,14 @@
             packed = jnp.where((lane16 >= 64 + g) & (lane16 < 64 + g + W), tail, packed)
     zsend[...] = packed
 
-    beside = sum(jnp.where(exists(step), 1, 0) for step in STEPS)
-    pl.semaphore_wait(barrier, beside + jnp.where(solid, rows_in, nb))
+    beside = sum(jnp.where(exists(step), 1, 0) for step in STEPS if step[1] <= 0)
+    pl.semaphore_wait(barrier, beside + jnp.where(solid, deep + lines - 1, 0))
+
+    @pl.when(solid)
+    def _():
+        for d in range(last):
+            for j in range(wide):
+                pl.semaphore_signal(ready, inc=1, device_id=(d, my_line * wide + j, slab), device_id_type=MESH)
 
     def halo_copies(sources, landings, ssem, rsem):
         return [
@@ -157,14 +162,25 @@
             for m, step in enumerate(STEPS)
         ]
 
-    def begin(copies):
+    everywhere = (-1, 0, 1)
+
+    def begin(copies, ways=everywhere):
         for m in reversed(range(len(STEPS))):
-            on(STEPS[m], copies[m].start)
+            if STEPS[m][1] in ways:
+                on(STEPS[m], copies[m].start)
+
+    def arrive(copies, ways):
+        for m, (db, dz) in enumerate(STEPS):
+            if dz in ways:
+                on((-db, -dz), copies[m].wait_recv)
+
+    def leave(copies):
+        for step, copy in zip(STEPS, copies):
+            on(step, copy.wait_send)
 
     def finish(copies):
-        for m, (db, dz) in enumerate(STEPS):
-            on((db, dz), copies[m].wait_send)
-            on((-db, -dz), copies[m].wait_recv)
+        arrive(copies, everywhere)
+        leave(copies)
 
     low, high = zsend.at[pl.ds(0, 8)], zsend.at[pl.ds(ROWS - 8, 8)]
     a_copies = halo_copies(
@@ -172,7 +188,7 @@
         [yst.at[0], yst.at[1], zst.at[0], zst.at[1]] + [dst8.at[i] for i in range(4)],
         a_send, a_recv,
     )
-    begin(a_copies)
+    begin(a_copies, (-1, 0))
 
     def sheet_copies(x, y, z, d, ssem, rsem):
         def part(r0, rn, c0, cn):
@@ -259,6 +275,13 @@
         for o in range(nb):
             meta_send[o, 0:1, :] = k[o:o + 1]
             meta_send[o, 1:2, :] = code[o:o + 1]
+
+    arrive(a_copies, (-1,))
+    begin(a_copies, (1,))
+
+    @pl.when(jnp.logical_not(solid))
+    def _():
+        pl.semaphore_wait(ready, wide)
 
         def send(i, _):
             to = far_first(lax.div(i, wide)) * wide + lax.rem(i, wide)
@@ -326,7 +349,8 @@
 
         hsum[...] = scatter(nb // group_p, group_p, lambda t: [t * group_p], packet_row, True)
 
-    finish(a_copies)
+    arrive(a_copies, (0, 1))
+    leave(a_copies)
     zr = jnp.concatenate([zst[0], ends(dst8[0], dst8[2], row8n)], axis=0)
     zl = jnp.concatenate([zst[1], ends(dst8[1], dst8[3], row8n)], axis=0)
     lane24 = iota((XR, 128), 1)
@@ -401,7 +425,7 @@
         )
 
     def line_in(t, ref, ssem, rsem):
-        line = lines - 1 - t
+        line = far_first(lines - 1 - t)
         whole(ref.at[pl.ds(line * deep, deep)], ssem, rsem.at[line]).wait_recv()
         return [line * deep]
 
@@ -420,24 +444,32 @@
         )
         begin(g_copies)
 
-    finish(u_copies)
-    unpack(ua, uy, uz, udg, LAYERS)
+    def written(first, count, m):
+        return pltpu.make_async_copy(
+            ua.at[pl.ds(first, count), pl.ds(0, ROWS), pl.ds(0, COLS)], out.at[pl.ds(first, count)], out_sem.at[m]
+        )
+
+    deeper, top = written(1, LAYERS - 1, 0), written(0, 1, 1)
 
     @pl.when(solid)
     def _():
+        sx[0, 0:ROWS, 0:COLS] = scatter(
+            lines, deep, lambda t: line_in(t, q_recv, q_ssem, q_rsem), lambda i: target_row(i, q_recv[i]), False
+        )
+        begin(s_copies)
+        finish(u_copies)
+        unpack(ua, uy, uz, udg, LAYERS)
         finish(g_copies)
         unpack(gx, gy, gz, gdg, 1)
         g = gx[0]
         inverse = 1.0 / (1.0 + g)
         gx[0] = g * inverse
-        sx[0, 0:ROWS, 0:COLS] = scatter(
-            lines, deep, lambda t: line_in(t, q_recv, q_ssem, q_rsem), lambda i: target_row(i, q_recv[i]), False
-        )
-        begin(s_copies)
         finish(s_copies)
         unpack(sx, sy, sz, sdg, 1)
         sx[0] = sx[0] * inverse
         phase(True)
+        deeper.start()
+        top.start()
         sheet = sheet_parts(ua[0, 0:ROWS, 0:COLS])
 
         def put(i, row):
@@ -461,7 +493,10 @@
 
     @pl.when(jnp.logical_not(solid))
     def _():
+        finish(u_copies)
+        unpack(ua, uy, uz, udg, LAYERS)
         phase(False)
+        deeper.start()
         whole(meta_send, meta_ssem, meta_rsem.at[0]).wait_send()
         whole(q_send, q_ssem, q_rsem.at[0]).wait_send()
 
@@ -482,10 +517,10 @@
         h = hsum[...]
         u = ua[0, 0:ROWS, 0:COLS]
         ua[0, 0:ROWS, 0:COLS] = u + (q - h * u) / (1.0 + h)
-
-    done = pltpu.make_async_copy(ua.at[own], out, out_sem)
-    done.start()
-    done.wait()
+        top.start()
+
+    deeper.wait()
+    top.wait()
 
 
 def body(nd, nb, ns, heat, ratio, courant, voxel, owner, target, link, tally):
@@ -503,7 +538,7 @@
     field = vm((LAYERS, XR, XC), F32)
     scratch = (
         [field] * 4 + [vm((1, XR, XC), F32)] * 2
-        + [vm((groups, 128), I32)] * 3 + [vm((groups, 128), F32)]
+        + [vm((groups, 128), I32)] * 3 + [vm((groups, 128), F32), vm((1, 1, 1), I32)]
         + [vm((2, LAYERS + 2, 8, COLS), F32), vm((ROWS, 128), F32)]
         + [vm((2, LAYERS + 2, 8, COLS), F32), vm((2, ROWS, 128), F32), vm((4, 8, 128), F32)]
         + stage(LAYERS) + stage(1) + stage(1)
@@ -512,21 +547,21 @@
         + [vm((nb, CAP), F32)] * 3 + [vm((ROWS, COLS), F32)]
         + [vm((nb, 2, CAP), F32), vm((nb, 1, CAP), F32), vm((rows_in, 2, CAP), F32), vm((rows_in, 1, CAP), F32)]
         + [vm((rows_in, 1, CAP), F32), vm((nb, 1, CAP), F32)]
-        + [sem((3,)), sem((4,)), sem]
+        + [sem((3,)), sem((5,)), sem((2,))]
         + [sem((8,))] * 8
-        + [sem, sem((lines,))] * 3
+        + [pltpu.SemaphoreType.REGULAR] + [sem, sem((lines,))] * 3
     )
     hbm = pl.BlockSpec(memory_space=pl.ANY)
     return pl.pallas_call(
         functools.partial(kernel, nd, nb, ns),
         out_shape=jax.ShapeDtypeStruct(heat.shape, F32),
-        in_specs=[hbm] * 7 + [pl.BlockSpec(memory_space=pltpu.SMEM)],
+        in_specs=[hbm] * 8,
         out_specs=hbm,
         scratch_shapes=scratch,
         compiler_params=pltpu.CompilerParams(
             collective_id=0, has_side_effects=True, vmem_limit_bytes=VMEM_BYTES
         ),
-    )(heat, ratio, courant, *slots, tally.reshape(1))
+    )(heat, ratio, courant, *slots, tally)
 
 
 def solution(mesh):

time: 48.8 us -> 47.3 us (0.969)
  Pallas kernels: 46 us -> 44.9 us
    pallas_call x1, Pallas kernels: 46 us -> 44.9 us  [body(): pl.pallas_call(functools.partial(kernel, nd, nb, ns), out_shape=jax.Shape...]
where the time goes in v3:
time: 47.3 us; the launch traced here: 47 us
  Pallas kernels  44.9 us (95%)
  local copies, waits for them, and re-layouts  1.47 us (3%)
  between operations  0.66 us (1%)
    pallas_call x1, Pallas kernels, body(): pl.pallas_call(functools.partial(kernel, nd, nb, ns), out_shape=jax.Shape...  44.9 us
    unnamed x1, local copies, waits for them, and re-layouts  1.47 us

profile of v3, /device:TPU:1, one launch (start us, length us, event | category | flops | bytes accessed | tf_op | source)
XLA Modules:
  0.0 47.0 jit_solution(7937388446053516222)
XLA Ops:
  0.7 44.9 %shard_map.82 = f32[4,16,256]{2,1,0:T(8,128)} custom-call(f32[4,16,256]{2,1,0:T(8,128)} %heat.1, f32[4,16,256]{2,1,0:T(8,128)} %ratio.1, f32[4,16,256]{2,1,0:T(8,128)} %courant.1, s32[16,128]{1,0:T(8,128)} %bitcast.4, s32[16,128]{1,0:T(8,128)} %bitcast.5, s32[16,128]{1,0:T(8,128)} %bitcast.6, f32[16,128]{1,0:T(8,128)} %bitcast.7, s32[1,1,1]{2,1,0:T(1,128)S(6)} %copy.10.tally_h), custom_call_target="tpu_custom_call" | custom-call | tf_op jit(solution)/shard_map/pallas_call | solution.py:555
  45.6 1.5 %copy.11 = f32[4,16,256]{2,1,0:T(8,128)} copy(f32[4,16,256]{2,1,0:T(8,128)} %shard_map.82) | data formatting | bytes 131072

commit v4 on v3

--- a/solution.py
+++ b/solution.py
@@ -10,12 +10,14 @@
 
 SWEEPS = 4
 W = 4
+HIGH, LOW = 32, 128
 CAP = 128
 VMEM_BYTES = 60 * 1024 * 1024
 LAYERS, ROWS, COLS = 4, 16, 256
 XR, XC = ROWS + 8, COLS + 128
 PARTS = 7
 STEPS = ((-1, 0), (1, 0), (0, -1), (0, 1), (-1, -1), (-1, 1), (1, -1), (1, 1))
+DOWN = (0, -1)
 MESH = pl.DeviceIdType.MESH
 F32, BF16, I32 = jnp.float32, jnp.bfloat16, jnp.int32
 NT = (((1,), (1,)), ((), ()))
@@ -42,11 +44,11 @@
     ua, ub, rx, cx, gx, sx,
     voxel, owner, target, link, tally,
     ysend, zsend, yst, zst, dst8,
-    uy, uz, udg, gy, gz, gdg, sy, sz, sdg,
+    uys, uzs, uy, uz, udg, gy, gz, gdg, sy, sz, sdg,
     hot, owner_hot, prefix, meta_a, meta_b,
-    cell_y, cell_z, link_p, hsum,
+    cell_high, cell_low, link_p, hsum,
     meta_send, q_send, meta_recv, q_recv, ans_send, wall_recv,
-    in_sem, slot_sem, out_sem,
+    in_sem, slot_sem,
     a_send, a_recv, u_send, u_recv, g_send, g_recv, s_send, s_recv,
     ready, meta_ssem, meta_rsem, q_ssem, q_rsem, ans_ssem, ans_rsem,
 ):
@@ -126,23 +128,26 @@
     for copy in fields:
         copy.wait()
     lane16 = iota((ROWS, 128), 1)
-    first, final = jnp.zeros((ROWS, 128), F32), jnp.zeros((ROWS, 128), F32)
-    packed = jnp.zeros((ROWS, 128), F32)
+
+    def pack(planes, rows, columns):
+        packed = jnp.zeros((ROWS, 128), F32)
+        for g, x in enumerate(planes):
+            half = slice(g % 2 * W, g % 2 * W + W)
+            rows[0, g // 2, half, :] = x[0:W]
+            rows[1, g // 2, half, :] = x[ROWS - W:]
+            at = g * W
+            head = pltpu.roll(x[:, 0:128], at, 1) if g else x[:, 0:128]
+            tail = pltpu.roll(x[:, 128:256], (64 + at + W) % 128, 1)
+            packed = jnp.where((lane16 >= at) & (lane16 < at + W), head, packed)
+            packed = jnp.where((lane16 >= 64 + at) & (lane16 < 64 + at + W), tail, packed)
+        columns[...] = packed
+
+    def plane(x, l):
+        return x[l, 0:ROWS, 0:COLS]
+
     for l in range(LAYERS):
-        c = cx[l, 0:ROWS, 0:COLS] * gas
-        cx[l, 0:ROWS, 0:COLS] = c
-        u, r = ua[l, 0:ROWS, 0:COLS], rx[l, 0:ROWS, 0:COLS]
-        ysend[0, l] = jnp.concatenate([u[0:W], r[0:W]], axis=0)
-        ysend[1, l] = jnp.concatenate([u[ROWS - W:], r[ROWS - W:]], axis=0)
-        ysend[0, LAYERS + l // 2, (l % 2) * W:(l % 2) * W + W, :] = c[0:W]
-        ysend[1, LAYERS + l // 2, (l % 2) * W:(l % 2) * W + W, :] = c[ROWS - W:]
-        for a, x in enumerate((u, r, c)):
-            g = (l * 3 + a) * W
-            head = pltpu.roll(x[:, 0:128], g, 1) if g else x[:, 0:128]
-            tail = pltpu.roll(x[:, 128:256], (64 + g + W) % 128, 1)
-            packed = jnp.where((lane16 >= g) & (lane16 < g + W), head, packed)
-            packed = jnp.where((lane16 >= 64 + g) & (lane16 < 64 + g + W), tail, packed)
-    zsend[...] = packed
+        cx[l, 0:ROWS, 0:COLS] = plane(cx, l) * gas
+    pack([plane(x, l) for l in range(LAYERS) for x in (ua, rx, cx)], ysend, zsend)
 
     beside = sum(jnp.where(exists(step), 1, 0) for step in STEPS if step[1] <= 0)
     pl.semaphore_wait(barrier, beside + jnp.where(solid, deep + lines - 1, 0))
@@ -169,63 +174,31 @@
             if STEPS[m][1] in ways:
                 on(STEPS[m], copies[m].start)
 
-    def arrive(copies, ways):
-        for m, (db, dz) in enumerate(STEPS):
-            if dz in ways:
-                on((-db, -dz), copies[m].wait_recv)
+    def arrive(copies, steps=STEPS):
+        for db, dz in steps:
+            on((-db, -dz), copies[STEPS.index((db, dz))].wait_recv)
 
     def leave(copies):
         for step, copy in zip(STEPS, copies):
             on(step, copy.wait_send)
 
     def finish(copies):
-        arrive(copies, everywhere)
+        arrive(copies)
         leave(copies)
 
-    low, high = zsend.at[pl.ds(0, 8)], zsend.at[pl.ds(ROWS - 8, 8)]
-    a_copies = halo_copies(
-        [ysend.at[0], ysend.at[1], zsend, zsend, low, low, high, high],
-        [yst.at[0], yst.at[1], zst.at[0], zst.at[1]] + [dst8.at[i] for i in range(4)],
-        a_send, a_recv,
-    )
-    begin(a_copies, (-1, 0))
-
-    def sheet_copies(x, y, z, d, ssem, rsem):
-        def part(r0, rn, c0, cn):
-            return x.at[:, pl.ds(r0, rn), pl.ds(c0, cn)]
-
+    def packed_copies(rows, columns, y, z, d, ssem, rsem):
+        head, tail = columns.at[pl.ds(0, 8)], columns.at[pl.ds(ROWS - 8, 8)]
         return halo_copies(
-            [
-                part(0, 8, 0, COLS), part(ROWS - 8, 8, 0, COLS),
-                part(0, ROWS, 0, 128), part(0, ROWS, COLS - 128, 128),
-                part(0, 8, 0, 128), part(0, 8, COLS - 128, 128),
-                part(ROWS - 8, 8, 0, 128), part(ROWS - 8, 8, COLS - 128, 128),
-            ],
+            [rows.at[0], rows.at[1], columns, columns, head, head, tail, tail],
             [y.at[0], y.at[1], z.at[0], z.at[1]] + [d.at[i] for i in range(4)],
             ssem, rsem,
         )
 
-    u_copies = sheet_copies(ua, uy, uz, udg, u_send, u_recv)
-    g_copies = sheet_copies(gx, gy, gz, gdg, g_send, g_recv)
-    s_copies = sheet_copies(sx, sy, sz, sdg, s_send, s_recv)
-
-    row8 = iota((8, COLS), 0)
-    row8n = iota((8, 128), 0)
-    lane8 = iota((8, 128), 1)
-
-    def sides(right, left, lanes):
-        return jnp.where(lanes < lanes_end, right, jnp.where(lanes >= lanes_from, left, 0.0))
-
-    def ends(after, prior, rows):
-        return jnp.where(rows < rows_end, after, jnp.where(rows >= rows_from, prior, 0.0))
-
-    def unpack(x, y, z, d, layers):
-        for l in range(layers):
-            x[l, ROWS:XR, 0:COLS] = ends(y[0, l], y[1, l], row8)
-            x[l, 0:ROWS, COLS:XC] = sides(z[0, l], z[1, l], lane16)
-            right = ends(d[0, l], d[2, l], row8n)
-            left = ends(d[1, l], d[3, l], row8n)
-            x[l, ROWS:XR, COLS:XC] = sides(right, left, lane8)
+    a_copies = packed_copies(ysend, zsend, yst, zst, dst8, a_send, a_recv)
+    begin(a_copies, (-1, 0))
+
+    def high_of(cell):
+        return (((cell >> 7) & 1) * ROWS + (cell >> 8)).astype(F32)
 
     @pl.when(jnp.logical_not(solid))
     def _():
@@ -258,7 +231,7 @@
             k1, rest = split2(k)
             k2, k3 = split2(rest)
             values = (
-                (v >> 8).astype(F32), (v & 255).astype(F32), (t >> 8).astype(F32), (t & 255).astype(F32),
+                high_of(v), (v & (LOW - 1)).astype(F32), high_of(t), (t & (LOW - 1)).astype(F32),
                 k1, k2, k3,
             )
             for q, value in enumerate(values):
@@ -268,44 +241,83 @@
         lax.fori_loop(0, groups, lay, jnp.zeros((nb, 128), F32))
         packet = dot(meta_a[...], meta_b[...], NT)
         part = [packet[q * nb:(q + 1) * nb] for q in range(PARTS)]
-        cell_y[...], cell_z[...] = part[0], part[1]
-        code = part[2] * 256.0 + part[3]
+        cell_high[...], cell_low[...] = part[0], part[1]
+        code = part[2] * float(LOW) + part[3]
         k = part[4] + part[5] + part[6]
         link_p[...] = k
         for o in range(nb):
             meta_send[o, 0:1, :] = k[o:o + 1]
             meta_send[o, 1:2, :] = code[o:o + 1]
 
-    arrive(a_copies, (-1,))
+    def sheet_copies(x, y, z, d, ssem, rsem):
+        def part(r0, rn, c0, cn):
+            return x.at[:, pl.ds(r0, rn), pl.ds(c0, cn)]
+
+        return halo_copies(
+            [
+                part(0, 8, 0, COLS), part(ROWS - 8, 8, 0, COLS),
+                part(0, ROWS, 0, 128), part(0, ROWS, COLS - 128, 128),
+                part(0, 8, 0, 128), part(0, 8, COLS - 128, 128),
+                part(ROWS - 8, 8, 0, 128), part(ROWS - 8, 8, COLS - 128, 128),
+            ],
+            [y.at[0], y.at[1], z.at[0], z.at[1]] + [d.at[i] for i in range(4)],
+            ssem, rsem,
+        )
+
+    u_copies = packed_copies(uys, uzs, uy, uz, udg, u_send, u_recv)
+    g_copies = sheet_copies(gx, gy, gz, gdg, g_send, g_recv)
+    s_copies = sheet_copies(sx, sy, sz, sdg, s_send, s_recv)
+
+    row8 = iota((8, COLS), 0)
+    row8n = iota((8, 128), 0)
+    lane8 = iota((8, 128), 1)
+
+    def sides(right, left, lanes):
+        return jnp.where(lanes < lanes_end, right, jnp.where(lanes >= lanes_from, left, 0.0))
+
+    def ends(after, prior, rows):
+        return jnp.where(rows < rows_end, after, jnp.where(rows >= rows_from, prior, 0.0))
+
+    def unpack_sheet(x, y, z, d):
+        x[0, ROWS:XR, 0:COLS] = ends(y[0, 0], y[1, 0], row8)
+        x[0, 0:ROWS, COLS:XC] = sides(z[0, 0], z[1, 0], lane16)
+        right = ends(d[0, 0], d[2, 0], row8n)
+        left = ends(d[1, 0], d[3, 0], row8n)
+        x[0, ROWS:XR, COLS:XC] = sides(right, left, lane8)
+
+    lane24 = iota((XR, 128), 1)
+
+    def unpack(planes, y, z, d):
+        right = jnp.concatenate([z[0], ends(d[0], d[2], row8n)], axis=0)
+        left = jnp.concatenate([z[1], ends(d[1], d[3], row8n)], axis=0)
+        for g, (x, l) in enumerate(planes):
+            after, prior = y[0, g // 2], y[1, g // 2]
+            if g % 2:
+                after = pltpu.roll(after, W, 0)
+            else:
+                prior = pltpu.roll(prior, W, 0)
+            x[l, ROWS:XR, 0:COLS] = ends(after, prior, row8)
+            at = g * W
+            x[l, :, COLS:XC] = sides(
+                pltpu.roll(right, 128 - at, 1) if g else right, pltpu.roll(left, 64 - W - at, 1), lane24
+            )
+
+    arrive(a_copies, [DOWN])
     begin(a_copies, (1,))
 
-    @pl.when(jnp.logical_not(solid))
-    def _():
-        pl.semaphore_wait(ready, wide)
-
-        def send(i, _):
-            to = far_first(lax.div(i, wide)) * wide + lax.rem(i, wide)
-            pltpu.make_async_remote_copy(
-                src_ref=meta_send.at[to], dst_ref=meta_recv.at[my_row],
-                send_sem=meta_ssem, recv_sem=meta_rsem.at[my_line], device_id=(last, to, slab), device_id_type=MESH,
-            ).start()
-            return 0
-
-        lax.fori_loop(0, nb, send, 0)
-
-    zrow = iota((COLS, 128), 0).astype(F32)
-    yrow = iota((ROWS, 128), 0).astype(F32)
-
-    def hot_columns(z):
-        return jnp.where(zrow == z, 1.0, 0.0).astype(BF16)
-
-    def spread(value, y):
+    low_row = iota((LOW, 128), 0).astype(F32)
+    high_row = iota((HIGH, 128), 0).astype(F32)
+
+    def hot_columns(at_low):
+        return jnp.where(low_row == at_low, 1.0, 0.0).astype(BF16)
+
+    def spread(value, at_high):
         a, b = split2(value)
-        there = yrow == y
+        there = high_row == at_high
         return jnp.concatenate([jnp.where(there, a, 0.0), jnp.where(there, b, 0.0)], axis=0).astype(BF16)
 
     def total(x):
-        return x[0:ROWS] + x[ROWS:2 * ROWS]
+        return x[0:HIGH] + x[HIGH:2 * HIGH]
 
     def scatter(steps, group, blocks_of, row_of, build):
         def step(t, acc):
@@ -313,10 +325,10 @@
             for first in blocks:
                 parts, hots = [], []
                 for j in range(group):
-                    value, y, z = row_of(first + j)
-                    parts.append(spread(value, y))
+                    value, at_high, at_low = row_of(first + j)
+                    parts.append(spread(value, at_high))
                     if build:
-                        hots.append(hot_columns(z))
+                        hots.append(hot_columns(at_low))
                 lane = pl.ds(pl.multiple_of(first * 128, 128), group * 128)
                 if build:
                     columns = jnp.concatenate(hots, axis=1)
@@ -326,16 +338,18 @@
                 acc = acc + dot(jnp.concatenate(parts, axis=1), columns, NT)
             return acc
 
-        return total(lax.fori_loop(0, steps, step, jnp.zeros((2 * ROWS, COLS), F32)))
+        sums = total(lax.fori_loop(0, steps, step, jnp.zeros((2 * HIGH, LOW), F32)))
+        return jnp.concatenate([sums[0:ROWS], sums[ROWS:HIGH]], axis=1)
 
     def sheet_parts(x):
+        x = jnp.concatenate([x[:, 0:LOW], x[:, LOW:COLS]], axis=0)
         return jnp.concatenate(split2(x), axis=0).astype(BF16)
 
-    def gather(sheet, first, group, y_of, put):
+    def gather(sheet, first, group, high_at, put):
         lane = pl.ds(pl.multiple_of(first * 128, 128), group * 128)
         got = total(dot(sheet, hot[:, lane], NN))
         for j in range(group):
-            here = jnp.where(yrow == y_of(first + j), got[:, j * 128:(j + 1) * 128], 0.0)
+            here = jnp.where(high_row == high_at(first + j), got[:, j * 128:(j + 1) * 128], 0.0)
             put(first + j, jnp.sum(here, axis=0, keepdims=True))
 
     pair = math.gcd(2, lines)
@@ -345,33 +359,27 @@
     def _():
         def packet_row(i):
             one = pl.ds(i, 1)
-            return link_p[one, :], cell_y[one, :], cell_z[one, :]
+            return link_p[one, :], cell_high[one, :], cell_low[one, :]
 
         hsum[...] = scatter(nb // group_p, group_p, lambda t: [t * group_p], packet_row, True)
 
-    arrive(a_copies, (0, 1))
+    @pl.when(jnp.logical_not(solid))
+    def _():
+        pl.semaphore_wait(ready, wide)
+
+        def send(i, _):
+            to = far_first(lax.div(i, wide)) * wide + lax.rem(i, wide)
+            pltpu.make_async_remote_copy(
+                src_ref=meta_send.at[to], dst_ref=meta_recv.at[my_row],
+                send_sem=meta_ssem, recv_sem=meta_rsem.at[my_line], device_id=(last, to, slab), device_id_type=MESH,
+            ).start()
+            return 0
+
+        lax.fori_loop(0, nb, send, 0)
+
+    arrive(a_copies, [step for step in STEPS if step != DOWN])
     leave(a_copies)
-    zr = jnp.concatenate([zst[0], ends(dst8[0], dst8[2], row8n)], axis=0)
-    zl = jnp.concatenate([zst[1], ends(dst8[1], dst8[3], row8n)], axis=0)
-    lane24 = iota((XR, 128), 1)
-    for l in range(LAYERS):
-        first_u, last_u = yst[0, l], yst[1, l]
-        first_c, last_c = yst[0, LAYERS + l // 2], yst[1, LAYERS + l // 2]
-        if l % 2:
-            first_c = pltpu.roll(first_c, W, 0)
-        else:
-            last_c = pltpu.roll(last_c, W, 0)
-        pairs = (
-            (ua, first_u, pltpu.roll(last_u, W, 0)),
-            (rx, pltpu.roll(first_u, W, 0), last_u),
-            (cx, first_c, last_c),
-        )
-        for a, (x, after, prior) in enumerate(pairs):
-            x[l, ROWS:XR, 0:COLS] = ends(after, prior, row8)
-            g = (l * 3 + a) * W
-            right = pltpu.roll(zr, 128 - g, 1) if g else zr
-            left = pltpu.roll(zl, 128 - W - 64 - g, 1)
-            x[l, :, COLS:XC] = sides(right, left, lane24)
+    unpack([(x, l) for l in range(LAYERS) for x in (ua, rx, cx)], yst, zst, dst8)
 
     def sweep(x, y, source):
         for l in range(LAYERS):
@@ -404,7 +412,7 @@
         def step(t, _):
             firsts = [far_first(t * pair + a) * wide for a in range(pair)]
             for first in firsts:
-                gather(sheet, first, wide, lambda i: cell_y[pl.ds(i, 1), :], put)
+                gather(sheet, first, wide, lambda i: cell_high[pl.ds(i, 1), :], put)
             for first in firsts:
                 for j in range(wide):
                     pltpu.make_async_remote_copy(
@@ -416,6 +424,7 @@
 
         lax.fori_loop(0, lines // pair, step, 0)
 
+    pack([plane(ua, l) for l in range(LAYERS)], uys, uzs)
     begin(u_copies)
 
     def whole(ref, ssem, rsem):
@@ -431,8 +440,8 @@
 
     def target_row(i, value):
         code = meta_recv[i, 1:2, :]
-        y = jnp.floor(code * (1.0 / 256.0))
-        return value, y, code - 256.0 * y
+        high = jnp.floor(code * (1.0 / LOW))
+        return value, high, code - float(LOW) * high
 
     @pl.when(solid)
     def _():
@@ -444,13 +453,6 @@
         )
         begin(g_copies)
 
-    def written(first, count, m):
-        return pltpu.make_async_copy(
-            ua.at[pl.ds(first, count), pl.ds(0, ROWS), pl.ds(0, COLS)], out.at[pl.ds(first, count)], out_sem.at[m]
-        )
-
-    deeper, top = written(1, LAYERS - 1, 0), written(0, 1, 1)
-
     @pl.when(solid)
     def _():
         sx[0, 0:ROWS, 0:COLS] = scatter(
@@ -458,18 +460,18 @@
         )
         begin(s_copies)
         finish(u_copies)
-        unpack(ua, uy, uz, udg, LAYERS)
+        unpack([(ua, l) for l in range(LAYERS)], uy, uz, udg)
         finish(g_copies)
-        unpack(gx, gy, gz, gdg, 1)
+        unpack_sheet(gx, gy, gz, gdg)
         g = gx[0]
         inverse = 1.0 / (1.0 + g)
         gx[0] = g * inverse
         finish(s_copies)
-        unpack(sx, sy, sz, sdg, 1)
+        unpack_sheet(sx, sy, sz, sdg)
         sx[0] = sx[0] * inverse
         phase(True)
-        deeper.start()
-        top.start()
+        for l in range(LAYERS):
+            out[l] = plane(ua, l)
         sheet = sheet_parts(ua[0, 0:ROWS, 0:COLS])
 
         def put(i, row):
@@ -494,15 +496,16 @@
     @pl.when(jnp.logical_not(solid))
     def _():
         finish(u_copies)
-        unpack(ua, uy, uz, udg, LAYERS)
+        unpack([(ua, l) for l in range(LAYERS)], uy, uz, udg)
         phase(False)
-        deeper.start()
+        for l in range(1, LAYERS):
+            out[l] = plane(ua, l)
         whole(meta_send, meta_ssem, meta_rsem.at[0]).wait_send()
         whole(q_send, q_ssem, q_rsem.at[0]).wait_send()
 
         def packet_row(i):
             one = pl.ds(i, 1)
-            return link_p[one, :] * wall_recv[i], cell_y[one, :], None
+            return link_p[one, :] * wall_recv[i], cell_high[one, :], None
 
         def lines_in(t):
             firsts = []
@@ -516,11 +519,7 @@
         q = scatter(lines // pair, wide, lines_in, packet_row, False)
         h = hsum[...]
         u = ua[0, 0:ROWS, 0:COLS]
-        ua[0, 0:ROWS, 0:COLS] = u + (q - h * u) / (1.0 + h)
-        top.start()
-
-    deeper.wait()
-    top.wait()
+        out[0] = u + (q - h * u) / (1.0 + h)
 
 
 def body(nd, nb, ns, heat, ratio, courant, voxel, owner, target, link, tally):
@@ -532,31 +531,34 @@
     vm = pltpu.VMEM
     sem = pltpu.SemaphoreType.DMA
 
-    def stage(layers):
-        return [vm((2, layers, 8, COLS), F32), vm((2, layers, ROWS, 128), F32), vm((4, layers, 8, 128), F32)]
+    def landings(planes):
+        return [vm((2, planes // 2, 8, COLS), F32), vm((2, ROWS, 128), F32), vm((4, 8, 128), F32)]
+
+    def packing(planes):
+        return [vm((2, planes // 2, 8, COLS), F32), vm((ROWS, 128), F32)]
+
+    sheet = [vm((2, 1, 8, COLS), F32), vm((2, 1, ROWS, 128), F32), vm((4, 1, 8, 128), F32)]
 
     field = vm((LAYERS, XR, XC), F32)
     scratch = (
         [field] * 4 + [vm((1, XR, XC), F32)] * 2
         + [vm((groups, 128), I32)] * 3 + [vm((groups, 128), F32), vm((1, 1, 1), I32)]
-        + [vm((2, LAYERS + 2, 8, COLS), F32), vm((ROWS, 128), F32)]
-        + [vm((2, LAYERS + 2, 8, COLS), F32), vm((2, ROWS, 128), F32), vm((4, 8, 128), F32)]
-        + stage(LAYERS) + stage(1) + stage(1)
-        + [vm((COLS, most * CAP), BF16), vm((groups * nb, 128), F32), vm((groups * nb, 256), F32)]
+        + packing(3 * LAYERS) + landings(3 * LAYERS) + packing(LAYERS) + landings(LAYERS) + sheet * 2
+        + [vm((LOW, most * CAP), BF16), vm((groups * nb, 128), F32), vm((groups * nb, 256), F32)]
         + [vm((PARTS * nb, groups * 128), BF16), vm((128, groups * 128), BF16)]
         + [vm((nb, CAP), F32)] * 3 + [vm((ROWS, COLS), F32)]
         + [vm((nb, 2, CAP), F32), vm((nb, 1, CAP), F32), vm((rows_in, 2, CAP), F32), vm((rows_in, 1, CAP), F32)]
         + [vm((rows_in, 1, CAP), F32), vm((nb, 1, CAP), F32)]
-        + [sem((3,)), sem((5,)), sem((2,))]
+        + [sem((3,)), sem((5,))]
         + [sem((8,))] * 8
         + [pltpu.SemaphoreType.REGULAR] + [sem, sem((lines,))] * 3
     )
     hbm = pl.BlockSpec(memory_space=pl.ANY)
     return pl.pallas_call(
         functools.partial(kernel, nd, nb, ns),
-        out_shape=jax.ShapeDtypeStruct(heat.shape, F32),
+        out_shape=pltpu.VMEM(heat.shape, F32),
         in_specs=[hbm] * 8,
-        out_specs=hbm,
+        out_specs=pl.BlockSpec(memory_space=pltpu.VMEM),
         scratch_shapes=scratch,
         compiler_params=pltpu.CompilerParams(
             collective_id=0, has_side_effects=True, vmem_limit_bytes=VMEM_BYTES

time: 47.3 us -> 42.9 us (0.907)
  Pallas kernels: 44.9 us -> 41.4 us
  local copies, waits for them, and re-layouts: 1.47 us -> 0.63 us
    pallas_call x1, Pallas kernels: 44.9 us -> 41.4 us  [body(): pl.pallas_call(functools.partial(kernel, nd, nb, ns), out_shape=pltpu.VME...]
    unnamed x1, local copies, waits for them, and re-layouts: 1.47 us -> 0.63 us
where the time goes in v4:
time: 42.9 us; the launch traced here: 42.7 us
  Pallas kernels  41.4 us (97%)
  between operations  0.66 us (2%)
  local copies, waits for them, and re-layouts  0.63 us (1%)
    pallas_call x1, Pallas kernels, body(): pl.pallas_call(functools.partial(kernel, nd, nb, ns), out_shape=pltpu.VME...  41.4 us

profile of v4, /device:TPU:1, one launch (start us, length us, event | category | flops | bytes accessed | tf_op | source)
XLA Modules:
  0.0 42.7 jit_solution(6019091148371938343)
XLA Ops:
  0.7 41.4 %shard_map.82 = f32[4,16,256]{2,1,0:T(8,128)S(1)} custom-call(f32[4,16,256]{2,1,0:T(8,128)} %heat.1, f32[4,16,256]{2,1,0:T(8,128)} %ratio.1, f32[4,16,256]{2,1,0:T(8,128)} %courant.1, s32[16,128]{1,0:T(8,128)} %bitcast.4, s32[16,128]{1,0:T(8,128)} %bitcast.5, s32[16,128]{1,0:T(8,128)} %bitcast.6, f32[16,128]{1,0:T(8,128)} %bitcast.7, ...), custom_call_target="tpu_custom_call" | custom-call | tf_op jit(solution)/shard_map/pallas_call | solution.py:557
  42.1 0.6 %copy.10 = f32[4,16,256]{2,1,0:T(8,128)} copy(f32[4,16,256]{2,1,0:T(8,128)S(1)} %shard_map.82) | data formatting | bytes 131072

commit v5 on v4

--- a/solution.py
+++ b/solution.py
@@ -357,11 +357,11 @@
 
     @pl.when(jnp.logical_not(solid))
     def _():
-        def packet_row(i):
-            one = pl.ds(i, 1)
-            return link_p[one, :], cell_high[one, :], cell_low[one, :]
-
-        hsum[...] = scatter(nb // group_p, group_p, lambda t: [t * group_p], packet_row, True)
+        def columns(i, _):
+            hot[:, pl.ds(pl.multiple_of(i * 128, 128), 128)] = hot_columns(cell_low[pl.ds(i, 1), :])
+            return 0
+
+        lax.fori_loop(0, nb, columns, 0, unroll=4)
 
     @pl.when(jnp.logical_not(solid))
     def _():
@@ -426,6 +426,14 @@
 
     pack([plane(ua, l) for l in range(LAYERS)], uys, uzs)
     begin(u_copies)
+
+    @pl.when(jnp.logical_not(solid))
+    def _():
+        def packet_row(i):
+            one = pl.ds(i, 1)
+            return link_p[one, :], cell_high[one, :], cell_low[one, :]
+
+        hsum[...] = scatter(nb // group_p, group_p, lambda t: [t * group_p], packet_row, False)
 
     def whole(ref, ssem, rsem):
         return pltpu.make_async_remote_copy(

time: 42.9 us -> 42.9 us (level)
  no operation moved by 1% of the time
where the time goes in v5:
time: 42.9 us; the launch traced here: 42.7 us
  Pallas kernels  41.4 us (97%)
  between operations  0.66 us (2%)
  local copies, waits for them, and re-layouts  0.63 us (1%)
    pallas_call x1, Pallas kernels, body(): pl.pallas_call(functools.partial(kernel, nd, nb, ns), out_shape=pltpu.VME...  41.4 us

profile of v5, /device:TPU:1, one launch (start us, length us, event | category | flops | bytes accessed | tf_op | source)
XLA Modules:
  0.0 42.7 jit_solution(14050237988410449014)
XLA Ops:
  0.7 41.4 %shard_map.82 = f32[4,16,256]{2,1,0:T(8,128)S(1)} custom-call(f32[4,16,256]{2,1,0:T(8,128)} %heat.1, f32[4,16,256]{2,1,0:T(8,128)} %ratio.1, f32[4,16,256]{2,1,0:T(8,128)} %courant.1, s32[16,128]{1,0:T(8,128)} %bitcast.4, s32[16,128]{1,0:T(8,128)} %bitcast.5, s32[16,128]{1,0:T(8,128)} %bitcast.6, f32[16,128]{1,0:T(8,128)} %bitcast.7, ...), custom_call_target="tpu_custom_call" | custom-call | tf_op jit(solution)/shard_map/pallas_call | solution.py:565
  42.1 0.6 %copy.10 = f32[4,16,256]{2,1,0:T(8,128)} copy(f32[4,16,256]{2,1,0:T(8,128)S(1)} %shard_map.82) | data formatting | bytes 131072
